TPU v7x, 256 devices: a whole 4x4x8 slice. The times are simulated.
256 devices in a mesh: row: 8 (over x, y_lo), col: 32 (over z, y_hi, core).
Axes of the slice: x: 4, y: 4 (y_hi: 2, y_lo: 2; y = y_hi * 2 + y_lo), z: 8, core: 2. Of those that a mesh axis runs over, the one named last changes fastest.
Arguments:
- hidden_in: bfloat16 [64, 256, 384], P('row', 'col'), may hold values from -6 to 6
- skip_input: bfloat16 [64, 256, 384], P('row', 'col'), may hold values from -6 to 6
- cache_frames: bfloat16 [2, 64, 256, 384], P(None, 'row', 'col'), may hold values from -3 to 3
- norm_gain: float32 [384], replicated, may hold values from 0.1 to 1.9
- conv_weight: bfloat16 [27, 384, 384], replicated, may hold values from -0.0625 to 0.0625
- conv_bias: float32 [384], replicated, may hold values from -3 to 3
- attn_gain: float32 [384], replicated, may hold values from 0.1 to 1.9
- w_qkv: bfloat16 [384, 1152], replicated, may hold values from -1 to 1
- b_qkv: float32 [1152], replicated, may hold values from -3 to 3
- w_proj: bfloat16 [384, 384], replicated, may hold values from -0.3125 to 0.3125
- b_proj: float32 [384], replicated, may hold values from -3 to 3
Outputs:
- block_out: bfloat16 [64, 256, 384], P('row', 'col')
All inputs are finite; a program needn't handle non-finite values.
Results may differ from a plain program's by a relative error of at most 0.02.
Values may be sent and summed in bfloat16 or wider, within the bound.
No kernel may reach another device: no remote copies, remote signals or barrier semaphores. Data moves between devices by JAX's collectives and lax.ppermute only.
A program may use at most 128 MiB of HBM per device.

v0:
```python
import math

import jax
import jax.numpy as jnp
from jax import lax
from jax.sharding import PartitionSpec as P


def extended(block, sides, width):
    for axis, dim in sides:
        count = lax.axis_size(axis)
        forward = [(i, i + 1) for i in range(count - 1)]
        backward = [(target, source) for source, target in forward]
        low = lax.ppermute(
            lax.slice_in_dim(block, block.shape[dim] - width, None, axis=dim), axis, forward
        )
        high = lax.ppermute(lax.slice_in_dim(block, 0, width, axis=dim), axis, backward)
        block = jnp.concatenate([low, block, high], axis=dim)
    return block


def rms_scale(values_in, gain_vec):
    floats = values_in.astype(jnp.float32)
    return floats * lax.rsqrt(jnp.mean(floats * floats, axis=-1, keepdims=True) + 1e-06) * gain_vec


def shards(
    hidden_in,
    skip_input,
    cache_frames,
    norm_gain,
    conv_weight,
    conv_bias,
    attn_gain,
    w_qkv,
    b_qkv,
    w_proj,
    b_proj,
):
    tile_rows, tile_cols, channels = hidden_in.shape
    pixels = tile_rows * tile_cols
    conv_in = jax.nn.silu(rms_scale(hidden_in, norm_gain)).astype(jnp.bfloat16)
    frames_in = jnp.concatenate([cache_frames, conv_in[None]], axis=0)
    padded = extended(frames_in, (("row", 1), ("col", 2)), 1)
    windows = []
    for frame_idx in range(3):
        for shift_row in range(3):
            for shift_col in range(3):
                windows.append(
                    padded[
                        frame_idx,
                        shift_row : shift_row + tile_rows,
                        shift_col : shift_col + tile_cols,
                    ]
                )
    patches = jnp.concatenate(windows, axis=-1).reshape(pixels, 27 * channels)
    conv_sum = (
        jnp.dot(
            patches,
            conv_weight.reshape(27 * channels, channels),
            preferred_element_type=jnp.float32,
        )
        + conv_bias
    )
    middle = (skip_input.reshape(pixels, channels).astype(jnp.float32) + conv_sum).astype(
        jnp.bfloat16
    )
    normed = rms_scale(middle, attn_gain).astype(jnp.bfloat16)
    queries = (
        jnp.dot(normed, w_qkv[:, :channels], preferred_element_type=jnp.float32) + b_qkv[:channels]
    ).astype(jnp.bfloat16)
    score_scale = 1.0 / math.sqrt(channels)
    key_value = (
        jnp.dot(normed, w_qkv[:, channels:], preferred_element_type=jnp.float32) + b_qkv[channels:]
    )
    key_local = key_value[:, :channels].astype(jnp.bfloat16)
    value_local = key_value[:, channels:].astype(jnp.bfloat16)
    top_score = jnp.full((pixels,), -1e30, jnp.float32)
    scores = (
        jnp.einsum(
            "qc,kc->qk",
            queries,
            lax.all_gather(key_local, ("row", "col"), axis=0, tiled=True),
            preferred_element_type=jnp.float32,
        )
        * score_scale
    )
    new_top = jnp.maximum(top_score, jnp.max(scores, axis=1))
    weights = jnp.exp(scores - new_top[:, None])
    denom = jnp.sum(weights, axis=1)
    accum = jnp.dot(
        weights.astype(jnp.bfloat16),
        lax.all_gather(value_local, ("row", "col"), axis=0, tiled=True),
        preferred_element_type=jnp.float32,
    )
    attended = (accum / denom[:, None]).astype(jnp.bfloat16)
    block_out = (
        middle.astype(jnp.float32)
        + jnp.dot(attended, w_proj, preferred_element_type=jnp.float32)
        + b_proj
    )
    return block_out.astype(jnp.bfloat16).reshape(tile_rows, tile_cols, channels)


def solution(mesh):
    return jax.shard_map(
        shards,
        mesh=mesh,
        in_specs=(
            P("row", "col", None),
            P("row", "col", None),
            P(None, "row", "col", None),
            P(),
            P(),
            P(),
            P(),
            P(),
            P(),
            P(),
            P(),
        ),
        out_specs=P("row", "col", None),
        check_vma=False,
    )
```

profile of v0, /device:TPU:32, one launch (start us, length us, event | category | flops | bytes accessed | tf_op | source)
XLA Modules:
  0.0 905.8 jit_solution(2500477411711950760)
XLA Ops:
  6.5 0.9 fusion.24
  7.5 0.9 fusion.36
  8.4 0.7 pad_maximum_fusion.10
  9.2 3.5 collective-permute-start
  12.6 1.3 collective-permute-start.1
  13.9 0.1 collective-permute-done
  14.1 4.2 collective-permute-done.1
  18.3 1.0 pad_maximum_fusion.5
  19.3 2.4 collective-permute-start.3
  21.7 2.0 collective-permute-start.2
  23.7 0.7 slice.167
  24.4 5.1 collective-permute-done.2
  29.5 1.2 pad_maximum_fusion
  30.7 0.0 copy-start.2
  30.7 0.0 copy-start.6
  30.8 0.0 copy-start.7
  31.2 0.3 copy-done.2
  31.5 0.1 constant_dynamic-update-slice_fusion.4
  31.7 0.0 copy-start.3
  31.7 0.0 slice-start
  31.7 4.8 multiply_reduce_fusion
  36.6 0.3 fusion.5
  36.9 0.6 fusion.37
  37.5 0.0 all-gather.3.cloned.1.call-update
  37.5 0.0 all-gather.5.cloned.1.call-start
  37.6 0.7 all-gather.5.cloned.1.call-update
  38.3 427.5 %all-gather.3.cloned.1.call-done = bf16[16384,384]{1,0:T(8,128)(2,1)} async-done(((bf16[64,384]{1,0:T(8,128)(2,1)}), bf16[16384,384]{1,0:T(8,128)(2,1)}) %all-gather.3.cloned.1.call-update) | async-done | bytes 12582928 | tf_op jit(solution)/shard_map/all_gather | solution.py:83
  465.7 10.9 %fusion.38 = (f32[64]{0:T(128)S(1)}, f32[64,16384]{1,0:T(8,128)}) fusion(bf16[16384,384]{1,0:T(8,128)(2,1)} %all-gather.3.cloned.1.call-done, bf16[384,1152]{1,0:T(8,128)(2,1)S(1)} %copy-done.3, f32[384]{0:T(512)S(1)} %slice-done, f32[64,384]{1,0:T(8,128)S(1)} %get-tuple-element.14, f32[384]{0:T(512)S(1)} %copy-done.5, f32[64]{0:T(128)S(1)} %add_rsqrt_fusion.1), kind=kOutput, calls=%fused_computation.104 | convolution fusion | flops 826400704 | bytes 17175296 | tf_op jit(solution)/shard_map/qc,kc->qk/dot_general | solution.py:80
  476.7 0.0 copy-start.8
  476.7 2.9 fusion
  479.6 410.5 %all-gather.5.cloned.1.call-done = bf16[16384,384]{1,0:T(8,128)(2,1)} async-done(((bf16[64,384]{1,0:T(8,128)(2,1)}), bf16[16384,384]{1,0:T(8,128)(2,1)}) %all-gather.5.cloned.1.call-update) | async-done | bytes 12582928 | tf_op jit(solution)/shard_map/all_gather | solution.py:93
  890.1 8.9 fusion.18
  (44 shorter events, 0.5 us)
Async XLA Ops:
  6.5 883.6 %copy-start = (bf16[384,384]{1,0:T(8,128)(2,1)S(1)}, bf16[384,384]{1,0:T(8,128)(2,1)}, u32[]{:S(2)}) copy-start(bf16[384,384]{1,0:T(8,128)(2,1)} %param.20) | copy-start | bytes 884740
  6.5 24.1 %copy-start.1 = (bf16[2,8,8,384]{3,2,1,0:T(8,128)(2,1)S(1)}, bf16[2,8,8,384]{3,2,1,0:T(8,128)(2,1)}, u32[]{:S(2)}) copy-start(bf16[2,8,8,384]{3,2,1,0:T(8,128)(2,1)} %param.13) | copy-start | bytes 294916
  6.5 459.2 %all-gather.3.cloned.1.call-start = ((), (), s32[]{:S(2)}) async-start(), calls=%async_computation | async-start | bytes 12632064 | tf_op jit(solution)/shard_map/all_gather | solution.py:83
  9.2 4.9 collective-permute-start
  12.6 5.7 collective-permute-start.1
  19.3 5.0 collective-permute-start.3
  21.7 7.8 collective-permute-start.2
  30.7 0.8 copy-start.2
  30.7 0.8 copy-start.6
  30.8 0.9 copy-start.4
  30.8 0.9 copy-start.7
  31.7 4.9 copy-start.3
  31.7 4.9 copy-start.5
  31.7 434.0 %slice-start = ((f32[1152]{0:T(1024)}), f32[384]{0:T(512)S(1)}, s32[]{:S(2)}) async-start(f32[1152]{0:T(1024)} %param.19), calls=%async_computation.2 | async-start | bytes 4096 | tf_op jit(solution)/shard_map/slice | solution.py:70
  37.5 852.6 %all-gather.5.cloned.1.call-start = ((), (), s32[]{:S(2)}) async-start(), calls=%async_computation.1 | async-start | bytes 12632064 | tf_op jit(solution)/shard_map/all_gather | solution.py:93
  476.7 413.4 %copy-start.8 = (f32[384]{0:T(512)S(1)}, f32[384]{0:T(512)}, u32[]{:S(2)}) copy-start(f32[384]{0:T(512)} %param.21) | copy-start | bytes 4612
Sparse Core Ops, SparseCore 0:
  37.6 428.0 all-gather.2
  467.6 422.4 all-gather.4
where the time goes:
time: 906 us
  waiting for transfers between devices  848 us (94%)
  matrix products  24.8 us (3%)
  between operations  13.7 us (2%)
  starting transfers between devices  9.13 us (1%)
    all_gather x1, waiting for transfers between devices, shards(): lax.all_gather(key_local, ('row', 'col'), axis=0, tiled=True)  427 us
    all_gather x1, waiting for transfers between devices, shards(): lax.all_gather(value_local, ('row', 'col'), axis=0, tiled=True)  411 us
  transfers between devices with their start and end apart: 6, of which 5 were waited for; matrix products, arithmetic and copies ran while one was open for 2% of the time, Pallas kernels for 0%

commit v1 on v0

v1 whole, which is shorter than its diff:
```python
import math

import jax
import jax.numpy as jnp
from jax import lax
from jax.experimental import pallas as pl
from jax.experimental.pallas import tpu as pltpu
from jax.sharding import Mesh
from jax.sharding import PartitionSpec as P

ROW = ("x", "ylo")
COL = ("z", "yhi", "core")
PLANE = ("x", "ylo", "yhi")
C = 384
TILE = 8
PIX = TILE * TILE
QUERIES = 16 * PIX
KEYS = 16 * PIX
SENDS = 4
LANES = 128
BF16 = jnp.bfloat16
F32 = jnp.float32


def pairs(count):
    inner = [(i, i ^ 1) for i in range(count)]
    outer = [(i, ((i + 1) ^ 1) - 1) for i in range(1, count - 1)]
    return inner, outer


def swapped(edges, axes):
    return [lax.ppermute(edge, axes, links) for edge, links in zip(edges, pairs(lax.axis_size(axes)))]


HBM = pl.BlockSpec(memory_space=pltpu.HBM)


def fetch(pairs_in, sems):
    copies = [
        pltpu.make_async_copy(source, target, sems.at[place])
        for place, (source, target) in enumerate(pairs_in)
    ]
    for copy in copies:
        copy.start()
    return copies


def arrive(copies):
    for copy in copies:
        copy.wait()


def row_kernel(cache, hidden, inner, outer, sems):
    odd = lax.axis_index("ylo")
    moves = []
    for edge, row in ((inner, 7 - 7 * odd), (outer, 7 * odd)):
        moves.append((cache.at[:, row], edge.at[pl.ds(0, 2)]))
        moves.append((hidden.at[row], edge.at[2]))
    arrive(fetch(moves, sems))


def row_edges(cache, hidden):
    edge = jax.ShapeDtypeStruct((3, TILE, C), BF16)
    return pl.pallas_call(
        row_kernel,
        in_specs=[HBM, HBM],
        out_shape=[edge, edge],
        scratch_shapes=[pltpu.SemaphoreType.DMA((4,))],
        compiler_params=pltpu.CompilerParams(vmem_limit_bytes=60 << 20),
    )(cache, hidden)


def side_kernel(cache, hidden, sides, wide):
    for frame in range(3):
        own = cache[frame] if frame < 2 else hidden[...]
        wide[frame] = own.astype(F32)
        for place, col in enumerate((0, TILE - 1)):
            sides[place, frame] = wide[frame, :, col, :].astype(BF16)


def own_sides(cache, hidden):
    return pl.pallas_call(
        side_kernel,
        out_shape=jax.ShapeDtypeStruct((2, 3, TILE, C), BF16),
        scratch_shapes=[pltpu.VMEM((3, TILE, TILE, C), F32)],
        compiler_params=pltpu.CompilerParams(vmem_limit_bytes=4 << 20),
        cost_estimate=pl.CostEstimate(flops=1 << 31, bytes_accessed=1 << 20, transcendentals=0),
    )(cache, hidden)


def column_kernel(sides, row_inner, row_outer, inner, outer):
    row_odd = lax.axis_index("ylo")
    odd = lax.axis_index("core")
    for frame in range(3):
        from_inner = row_inner[frame].astype(F32)
        from_outer = row_outer[frame].astype(F32)
        above = jnp.where(row_odd == 1, from_inner, from_outer)
        below = jnp.where(row_odd == 1, from_outer, from_inner)
        left, right = [
            jnp.concatenate(
                [above[col : col + 1], sides[place, frame].astype(F32), below[col : col + 1]], axis=0
            )
            for place, col in enumerate((0, TILE - 1))
        ]
        inner[frame] = jnp.where(odd == 1, left, right).astype(BF16)
        outer[frame] = jnp.where(odd == 1, right, left).astype(BF16)


def column_edges(sides, row_inner, row_outer):
    edge = jax.ShapeDtypeStruct((3, TILE + 2, C), BF16)
    return pl.pallas_call(
        column_kernel,
        out_shape=[edge, edge],
        compiler_params=pltpu.CompilerParams(vmem_limit_bytes=4 << 20),
        cost_estimate=pl.CostEstimate(flops=1 << 34, bytes_accessed=1 << 20, transcendentals=0),
    )(sides, row_inner, row_outer)


def rms(floats, gain):
    return floats * lax.rsqrt(jnp.mean(floats * floats, axis=-1, keepdims=True) + 1e-06) * gain


def conv_kernel(
    cache, hidden, row_inner, row_outer, col_inner, col_outer, weight, skip,
    norm_gain, conv_bias, attn_gain, w_qkv, b_qkv, middle, normed, queries, wide, shifted,
):
    row_odd = lax.axis_index("ylo")
    odd = lax.axis_index("core")
    total = jnp.zeros((PIX, C), F32)
    for frame in range(3):
        own = cache[frame] if frame < 2 else hidden[...]
        wide[pl.ds(1, TILE), 1 : 1 + TILE] = own.astype(F32)
        wide[9 - 9 * row_odd, 1 : 1 + TILE] = row_inner[frame].astype(F32)
        wide[9 * row_odd, 1 : 1 + TILE] = row_outer[frame].astype(F32)
        from_inner = col_inner[frame].astype(F32)
        from_outer = col_outer[frame].astype(F32)
        wide[:, 0] = jnp.where(odd == 1, from_inner, from_outer)
        wide[:, 1 + TILE] = jnp.where(odd == 1, from_outer, from_inner)
        block = wide[:, 0 : TILE + 2]
        if frame == 2:
            block = rms(block, norm_gain[...].reshape(1, 1, C))
            block = (block * jax.nn.sigmoid(block)).astype(BF16).astype(F32)
        for col in range(3):
            shifted[frame, col] = block[:, col : col + TILE, :]
    for frame in range(3):
        for row in range(3):
            tap = 9 * frame + 3 * row
            window = jnp.concatenate(
                [
                    shifted[frame, col, row : row + TILE].reshape(PIX, C).astype(BF16)
                    for col in range(3)
                ],
                axis=1,
            )
            total += jnp.dot(
                window, weight[tap * C : (tap + 3) * C], preferred_element_type=F32
            )
    mid = (skip[...].astype(F32) + (total + conv_bias[...])).astype(BF16)
    middle[...] = mid
    norm = rms(mid.astype(F32), attn_gain[...]).astype(BF16)
    normed[...] = norm
    query = (jnp.dot(norm, w_qkv[:, :C], preferred_element_type=F32) + b_qkv[:C]).astype(BF16)
    for place in range(16):
        queries[place * PIX : (place + 1) * PIX] = query


def conv_stage(cache, hidden, rows, cols, weight, skip, norm_gain, conv_bias, attn_gain, w_qkv, b_qkv):
    out = jax.ShapeDtypeStruct((PIX, C), BF16)
    return pl.pallas_call(
        conv_kernel,
        out_shape=[out, out, jax.ShapeDtypeStruct((QUERIES, C), BF16)],
        scratch_shapes=[
            pltpu.VMEM((TILE + 2, 2 * TILE, C), F32),
            pltpu.VMEM((3, 3, TILE + 2, TILE, C), F32),
        ],
        compiler_params=pltpu.CompilerParams(vmem_limit_bytes=24 << 20),
    )(cache, hidden, *rows, *cols, weight, skip, norm_gain, conv_bias, attn_gain, w_qkv, b_qkv)


def pair_kernel(own, far, both):
    both[:PIX] = own[...]
    both[PIX:] = far[...]


def pair_stage(own, far):
    return pl.pallas_call(
        pair_kernel,
        out_shape=jax.ShapeDtypeStruct((2 * PIX, C), BF16),
        compiler_params=pltpu.CompilerParams(vmem_limit_bytes=4 << 20),
        cost_estimate=pl.CostEstimate(flops=1 << 34, bytes_accessed=1 << 20, transcendentals=0),
    )(own, far)


def split3(value):
    first = value.astype(BF16)
    rest = value - first.astype(F32)
    second = rest.astype(BF16)
    third = (rest - second.astype(F32)).astype(BF16)
    return first.astype(F32), second.astype(F32), third.astype(F32)


def attend_kernel(queries, line, other, w_qkv, b_qkv, partial):
    normed = jnp.concatenate([line[...], other[...]], axis=0)
    projected = jnp.dot(normed, w_qkv[:, C:], preferred_element_type=F32) + b_qkv[C:]
    key_block = projected[:, :C].astype(BF16)
    values = projected[:, C:].astype(BF16).T
    scores = lax.dot_general(
        key_block, queries[...], (((1,), (1,)), ((), ())), preferred_element_type=F32
    ) * (math.log2(math.e) / math.sqrt(C))
    top = jnp.max(scores, axis=0, keepdims=True)
    weights = jnp.exp2(scores - top)
    denom = jnp.sum(weights, axis=0, keepdims=True)
    weights = weights.astype(BF16)
    parts = split3(top) + split3(denom)
    stats = jnp.concatenate(parts + (jnp.zeros((2, QUERIES), F32),), axis=0)
    for place in range(SENDS):
        group = QUERIES // SENDS
        numer = jnp.dot(
            values, weights[:, place * group : (place + 1) * group], preferred_element_type=F32
        ).T.astype(BF16)
        first = place * group // PIX
        for index in range(group // PIX):
            low = (first + index) * PIX
            for part in range(3):
                partial[first + index, part * PIX : (part + 1) * PIX] = numer[
                    index * PIX : (index + 1) * PIX, part * LANES : (part + 1) * LANES
                ]
            partial[first + index, 3 * PIX :] = jnp.concatenate(
                [stats[:, low : low + PIX], jnp.zeros((8, LANES - PIX), F32)], axis=1
            ).astype(BF16)


def attend_stage(queries, line, other, w_qkv, b_qkv):
    return pl.pallas_call(
        attend_kernel,
        out_shape=jax.ShapeDtypeStruct((16, 3 * PIX + 8, LANES), BF16),
        compiler_params=pltpu.CompilerParams(vmem_limit_bytes=40 << 20),
    )(queries, line, other, w_qkv, b_qkv)


def finish_kernel(partials, middle, w_proj, b_proj, block_out):
    stats = partials[:, 3 * PIX :].astype(F32)
    tops = stats[:, 0] + stats[:, 1] + stats[:, 2]
    denoms = stats[:, 3] + stats[:, 4] + stats[:, 5]
    scales = jnp.exp2(tops - jnp.max(tops, axis=0, keepdims=True))
    shares = (scales / jnp.maximum(jnp.sum(scales * denoms, axis=0, keepdims=True), 0.5)).T
    attended = jnp.concatenate(
        [
            sum(
                shares[:PIX, source : source + 1]
                * partials[source, part * PIX : (part + 1) * PIX].astype(F32)
                for source in range(16)
            )
            for part in range(3)
        ],
        axis=1,
    )
    block_out[...] = (
        middle[...].astype(F32)
        + jnp.dot(attended.astype(BF16), w_proj[...], preferred_element_type=F32)
        + b_proj[...]
    ).astype(BF16)


def finish_stage(partials, middle, w_proj, b_proj):
    return pl.pallas_call(
        finish_kernel,
        out_shape=jax.ShapeDtypeStruct((PIX, C), BF16),
        compiler_params=pltpu.CompilerParams(vmem_limit_bytes=8 << 20),
    )(partials, middle, w_proj, b_proj)


def steps(hop, count=8):
    return [(i, (i + hop) % count) for i in range(count)]


def flips(mask, count=8):
    return [(i, i ^ mask) for i in range(count)]


def shards(
    hidden_in,
    skip_input,
    cache_frames,
    norm_gain,
    conv_weight,
    conv_bias,
    attn_gain,
    w_qkv,
    b_qkv,
    w_proj,
    b_proj,
):
    rows = swapped(row_edges(cache_frames, hidden_in), ROW)
    cols = swapped(column_edges(own_sides(cache_frames, hidden_in), *rows), COL)
    middle, normed, queries = conv_stage(
        cache_frames,
        hidden_in,
        rows,
        cols,
        conv_weight.reshape(27 * C, C),
        skip_input.reshape(PIX, C),
        norm_gain,
        conv_bias,
        attn_gain,
        w_qkv,
        b_qkv,
    )
    all_queries = lax.all_to_all(queries, PLANE, 0, 0, tiled=True)
    far = pair_stage(normed, lax.ppermute(normed, "z", flips(4)))
    own_line = jnp.concatenate([far] + [lax.ppermute(far, "z", links) for links in (flips(2), steps(1), steps(-1))], axis=0)
    other_line = lax.ppermute(own_line, "core", flips(1, 2))
    partial = attend_stage(all_queries, own_line, other_line, w_qkv, b_qkv)
    partials = lax.all_to_all(partial, PLANE, 0, 0, tiled=True)
    block_out = finish_stage(partials, middle, w_proj, b_proj)
    return block_out.reshape(TILE, TILE, C)


def solution(mesh):
    fine = Mesh(mesh.devices.reshape(4, 2, 8, 2, 2), ROW + COL)
    return jax.shard_map(
        shards,
        mesh=fine,
        in_specs=(
            P(ROW, COL, None),
            P(ROW, COL, None),
            P(None, ROW, COL, None),
            P(),
            P(),
            P(),
            P(),
            P(),
            P(),
            P(),
            P(),
        ),
        out_specs=P(ROW, COL, None),
        check_vma=False,
    )
```

time: 906 us -> 72.6 us (0.08)
  waiting for transfers between devices: 848 us -> 14.6 us
  matrix products: 24.8 us -> 0 us
  starting transfers between devices: 9.13 us -> 28.2 us
  blocking collectives: 0 us -> 18.5 us
  between operations: 13.7 us -> 0.28 us
    all_gather x2 -> x0, waiting for transfers between devices: 838 us -> none  [the longest x1 427 us: shards(): lax.all_gather(key_local, ('row', 'col'), axis=0, tiled=True)]
    dot_general x4 -> x0, matrix products: 24.8 us -> none  [the longest x1 10.9 us: shards(): jnp.einsum('qc,kc->qk', queries, lax.all_gather(key_local, ('row', 'col')...]
    all_to_all x0 -> x1, blocking collectives: none -> 18.5 us  [shards(): partials = lax.all_to_all(partial, PLANE, 0, 0, tiled=True)]
    all_to_all x0 -> x1, starting transfers between devices: none -> 9.77 us  [shards(): all_queries = lax.all_to_all(queries, PLANE, 0, 0, tiled=True)]
    ppermute x4 -> x9, starting transfers between devices: 9.09 us -> 18.4 us  [the longest x4 7.22 us: swapped(): lax.ppermute(edge, axes, links)]
  transfers between devices with their start and end apart: 6 -> 10, of which waited for: 5 -> 6; matrix products, arithmetic and copies ran while one was open for 2% -> 0% of each run, Pallas kernels for 0% -> 0%
where the time goes in v1:
time: 72.6 us; the launch traced here: 72.1 us
  starting transfers between devices  28.2 us (39%)
  blocking collectives  18.5 us (25%)
  waiting for transfers between devices  14.6 us (20%)
  Pallas kernels  8.72 us (12%)
  local copies, waits for them, and re-layouts  1.76 us (2%)
    all_to_all x1, blocking collectives, shards(): partials = lax.all_to_all(partial, PLANE, 0, 0, tiled=True)  18.5 us
    all_to_all x1, starting transfers between devices, shards(): all_queries = lax.all_to_all(queries, PLANE, 0, 0, tiled=True)  9.77 us
    ppermute x4, starting transfers between devices, swapped(): lax.ppermute(edge, axes, links)  7.22 us
    ppermute x1, starting transfers between devices, shards(): far = pair_stage(normed, lax.ppermute(normed, 'z', flips(4)))  6.29 us
    all_to_all x1, waiting for transfers between devices, shards(): all_queries = lax.all_to_all(queries, PLANE, 0, 0, tiled=True)  5.52 us
    ppermute x3, starting transfers between devices, shards(): lax.ppermute(far, 'z', links)  4.79 us
    ppermute x3, waiting for transfers between devices, shards(): lax.ppermute(far, 'z', links)  4.18 us
    pallas_call x1, Pallas kernels, attend_stage(): pl.pallas_call(attend_kernel, out_shape=jax.ShapeDtypeStruct((16, 3 * PIX...  3.37 us
  transfers between devices with their start and end apart: 10, of which 6 were waited for; matrix products, arithmetic and copies ran while one was open for 0% of the time, Pallas kernels for 0%

profile of v1, /device:TPU:32, one launch (start us, length us, event | category | flops | bytes accessed | tf_op | source)
XLA Modules:
  0.0 72.1 jit_solution(9367359687939426028)
XLA Ops:
  0.0 1.4 %shard_map.109 = (bf16[3,8,384]{2,1,0:T(8,128)(2,1)}, bf16[3,8,384]{2,1,0:T(8,128)(2,1)}) custom-call(bf16[2,8,8,384]{3,2,1,0:T(8,128)(2,1)} %cache.5, bf16[8,8,384]{2,1,0:T(8,128)(2,1)} %hidden.5), custom_call_target="tpu_custom_call" | custom-call | tf_op jit(solution)/shard_map/pallas_call | solution.py:64
  1.4 1.7 %collective-permute-start = (bf16[3,8,384]{2,1,0:T(8,128)(2,1)}, bf16[3,8,384]{2,1,0:T(8,128)(2,1)S(1)}, u32[]{:S(2)}, u32[]{:S(2)}) collective-permute-start(bf16[3,8,384]{2,1,0:T(8,128)(2,1)} %get-tuple-element.12), channel_id=1, source_target_pairs={{0,32},{32,0},{64,96},{96,64},{128,160},{160,128},{192,224},{224,1... | collective-permute-start | bytes 55304 | tf_op jit(solution)/shard_map/ppermute | solution.py:32
  3.1 0.7 collective-permute-start.1
  3.7 0.0 copy-start.1
  3.7 0.9 %copy-done.1 = bf16[2,8,8,384]{3,2,1,0:T(8,128)(2,1)S(1)} copy-done((bf16[2,8,8,384]{3,2,1,0:T(8,128)(2,1)S(1)}, bf16[2,8,8,384]{3,2,1,0:T(8,128)(2,1)}, u32[]{:S(2)}) %copy-start.1) | copy-done | bytes 98328
  4.6 0.8 %copy-done.4 = bf16[8,8,384]{2,1,0:T(8,128)(2,1)S(1)} copy-done((bf16[8,8,384]{2,1,0:T(8,128)(2,1)S(1)}, bf16[8,8,384]{2,1,0:T(8,128)(2,1)}, u32[]{:S(2)}) %copy-start.4) | copy-done | bytes 49176
  5.4 0.1 shard_map.110.sides
  5.5 0.0 slice-start.1
  5.5 0.0 copy-start
  5.6 0.0 copy-start.6
  5.6 0.0 copy-start.7
  5.6 0.0 copy-start.9
  5.6 0.0 copy-start.10
  5.7 0.1 collective-permute-start.2
  5.8 4.8 %collective-permute-start.3 = (bf16[3,10,384]{2,1,0:T(8,128)(2,1)S(1)}, bf16[3,10,384]{2,1,0:T(8,128)(2,1)S(1)}, u32[]{:S(2)}, u32[]{:S(2)}) collective-permute-start(bf16[3,10,384]{2,1,0:T(8,128)(2,1)S(1)} %get-tuple-element.15), channel_id=1, source_target_pairs={{1,2},{2,1},{3,4},{4,3},{5,6},{6,5},{7,8},{8,7},{9,10},{10,9},{11,... | collective-permute-start | bytes 69128 | tf_op jit(solution)/shard_map/ppermute | solution.py:32
  10.6 3.2 %collective-permute-done.3.col_outer = bf16[3,10,384]{2,1,0:T(8,128)(2,1)S(1)} collective-permute-done((bf16[3,10,384]{2,1,0:T(8,128)(2,1)S(1)}, bf16[3,10,384]{2,1,0:T(8,128)(2,1)S(1)}, u32[]{:S(2)}, u32[]{:S(2)}) %collective-permute-start.3) | collective-permute-done | bytes 23072 | tf_op jit(solution)/shard_map/ppermute | solution.py:32
  13.9 2.6 %shard_map.112 = (bf16[64,384]{1,0:T(8,128)(2,1)S(1)}, bf16[64,384]{1,0:T(8,128)(2,1)S(1)}, bf16[1024,384]{1,0:T(8,128)(2,1)}) custom-call(bf16[2,8,8,384]{3,2,1,0:T(8,128)(2,1)S(1)} %copy-done.2, bf16[8,8,384]{2,1,0:T(8,128)(2,1)S(1)} %copy-done.5, bf16[3,8,384]{2,1,0:T(8,128)(2,1)S(1)} %collective-permute-done.row_inner, ...), custom_call_target="tpu_custom_call" | custom-call | tf_op jit(solution)/shard_map/pallas_call | solution.py:169
  16.5 6.3 %collective-permute-start.4 = (bf16[64,384]{1,0:T(8,128)(2,1)S(1)}, bf16[64,384]{1,0:T(8,128)(2,1)S(1)}, u32[]{:S(2)}, u32[]{:S(2)}) collective-permute-start(bf16[64,384]{1,0:T(8,128)(2,1)S(1)} %get-tuple-element.17.own), channel_id=1, source_target_pairs={{0,16},{4,20},{8,24},{12,28},{16,0},{20,4},{24,8},{28,12},{1,17},{... | collective-permute-start | bytes 147464 | tf_op jit(solution)/shard_map/ppermute | solution.py:310
  22.8 9.8 %all-to-all-start = ((bf16[16,64,384]{2,1,0:T(8,128)(2,1)}), bf16[16,64,384]{2,1,0:T(8,128)(2,1)S(1)}, u32[]{:S(2)}, u32[]{:S(2)}) async-start(bf16[16,64,384]{2,1,0:T(8,128)(2,1)} %bitcast.2), calls=%async_computation | async-start | bytes 1572864 | tf_op jit(solution)/shard_map/all_to_all | solution.py:309
  32.6 0.0 copy-start.3
  32.7 1.1 %collective-permute-start.7 = (bf16[128,384]{1,0:T(8,128)(2,1)S(1)}, bf16[128,384]{1,0:T(8,128)(2,1)S(1)}, u32[]{:S(2)}, u32[]{:S(2)}) collective-permute-start(bf16[128,384]{1,0:T(8,128)(2,1)S(1)} %shard_map.113), channel_id=1, source_target_pairs={{0,28},{4,0},{8,4},{12,8},{16,12},{20,16},{24,20},{28,24},{1,29},{... | collective-permute-start | bytes 294920 | tf_op jit(solution)/shard_map/ppermute | solution.py:311
  33.8 1.0 %collective-permute-start.6 = (bf16[128,384]{1,0:T(8,128)(2,1)S(1)}, bf16[128,384]{1,0:T(8,128)(2,1)S(1)}, u32[]{:S(2)}, u32[]{:S(2)}) collective-permute-start(bf16[128,384]{1,0:T(8,128)(2,1)S(1)} %shard_map.113), channel_id=1, source_target_pairs={{0,4},{4,8},{8,12},{12,16},{16,20},{20,24},{24,28},{28,0},{1,5},{5... | collective-permute-start | bytes 294920 | tf_op jit(solution)/shard_map/ppermute | solution.py:311
  34.8 2.7 %collective-permute-start.5 = (bf16[128,384]{1,0:T(8,128)(2,1)S(1)}, bf16[128,384]{1,0:T(8,128)(2,1)S(1)}, u32[]{:S(2)}, u32[]{:S(2)}) collective-permute-start(bf16[128,384]{1,0:T(8,128)(2,1)S(1)} %shard_map.113), channel_id=1, source_target_pairs={{0,8},{4,12},{8,0},{12,4},{16,24},{20,28},{24,16},{28,20},{1,9},{5... | collective-permute-start | bytes 294920 | tf_op jit(solution)/shard_map/ppermute | solution.py:311
  37.5 0.8 %collective-permute-done.7 = bf16[128,384]{1,0:T(8,128)(2,1)S(1)} collective-permute-done((bf16[128,384]{1,0:T(8,128)(2,1)S(1)}, bf16[128,384]{1,0:T(8,128)(2,1)S(1)}, u32[]{:S(2)}, u32[]{:S(2)}) %collective-permute-start.7) | collective-permute-done | bytes 98336 | tf_op jit(solution)/shard_map/ppermute | solution.py:311
  38.2 1.1 %collective-permute-done.6 = bf16[128,384]{1,0:T(8,128)(2,1)S(1)} collective-permute-done((bf16[128,384]{1,0:T(8,128)(2,1)S(1)}, bf16[128,384]{1,0:T(8,128)(2,1)S(1)}, u32[]{:S(2)}, u32[]{:S(2)}) %collective-permute-start.6) | collective-permute-done | bytes 98336 | tf_op jit(solution)/shard_map/ppermute | solution.py:311
  39.4 2.3 %collective-permute-done.5 = bf16[128,384]{1,0:T(8,128)(2,1)S(1)} collective-permute-done((bf16[128,384]{1,0:T(8,128)(2,1)S(1)}, bf16[128,384]{1,0:T(8,128)(2,1)S(1)}, u32[]{:S(2)}, u32[]{:S(2)}) %collective-permute-start.5) | collective-permute-done | bytes 98336 | tf_op jit(solution)/shard_map/ppermute | solution.py:311
  41.7 0.1 collective-permute-start.8
  41.8 1.7 %collective-permute-done.8.other = bf16[512,384]{1,0:T(8,128)(2,1)S(1)} collective-permute-done((bf16[512,384]{1,0:T(8,128)(2,1)S(1)}, bf16[512,384]{1,0:T(8,128)(2,1)S(1)}, u32[]{:S(2)}, u32[]{:S(2)}) %collective-permute-start.8) | collective-permute-done | bytes 393248 | tf_op jit(solution)/shard_map/ppermute | solution.py:312
  43.5 5.5 %all-to-all-done = bf16[16,64,384]{2,1,0:T(8,128)(2,1)S(1)} async-done(((bf16[16,64,384]{2,1,0:T(8,128)(2,1)}), bf16[16,64,384]{2,1,0:T(8,128)(2,1)S(1)}, u32[]{:S(2)}, u32[]{:S(2)}) %all-to-all-start) | async-done | bytes 786464 | tf_op jit(solution)/shard_map/all_to_all | solution.py:309
  49.0 3.4 %shard_map.114 = bf16[16,200,128]{2,1,0:T(8,128)(2,1)S(1)} custom-call(bf16[1024,384]{1,0:T(8,128)(2,1)S(1)} %bitcast.8, bf16[512,384]{1,0:T(8,128)(2,1)S(1)} %pad_maximum_fusion.line, bf16[512,384]{1,0:T(8,128)(2,1)S(1)} %collective-permute-done.8.other, bf16[384,1152]{1,0:T(8,128)(2,1)S(1)} %copy-done, f32[1152]{0:T(1024)S(1)} %copy-done.7), custom_call_target="tpu_custom_call" | custom-call | tf_op jit(solution)/shard_map/pallas_call | solution.py:234
  52.4 18.5 %all_to_all.16.partials = bf16[16,200,128]{2,1,0:T(8,128)(2,1)S(1)} all-to-all(bf16[16,200,128]{2,1,0:T(8,128)(2,1)S(1)} %shard_map.114), channel_id=1, replica_groups=mesh['x'=4,'ylo'=2,'z'=8,'yhi'=2,'core'=2] {'x','ylo','yhi'}, dimensions={0} | all-to-all | bytes 1638400 | tf_op jit(solution)/shard_map/all_to_all | solution.py:314
  70.9 1.2 %shard_map.115 = bf16[64,384]{1,0:T(8,128)(2,1)} custom-call(bf16[16,200,128]{2,1,0:T(8,128)(2,1)S(1)} %all_to_all.16.partials, bf16[64,384]{1,0:T(8,128)(2,1)S(1)} %get-tuple-element.18.middle, bf16[384,384]{1,0:T(8,128)(2,1)S(1)} %copy-done.3, f32[384]{0:T(512)S(1)} %copy-done.11), custom_call_target="tpu_custom_call" | custom-call | tf_op jit(solution)/shard_map/pallas_call | solution.py:266
  (26 shorter events, 0.1 us)
Async XLA Ops:
  1.4 4.2 %collective-permute-start = (bf16[3,8,384]{2,1,0:T(8,128)(2,1)}, bf16[3,8,384]{2,1,0:T(8,128)(2,1)S(1)}, u32[]{:S(2)}, u32[]{:S(2)}) collective-permute-start(bf16[3,8,384]{2,1,0:T(8,128)(2,1)} %get-tuple-element.12), channel_id=1, source_target_pairs={{0,32},{32,0},{64,96},{96,64},{128,160},{160,128},{192,224},{224,1... | collective-permute-start | bytes 55304 | tf_op jit(solution)/shard_map/ppermute | solution.py:32
  3.1 2.6 %collective-permute-start.1 = (bf16[3,8,384]{2,1,0:T(8,128)(2,1)}, bf16[3,8,384]{2,1,0:T(8,128)(2,1)S(1)}, u32[]{:S(2)}, u32[]{:S(2)}) collective-permute-start(bf16[3,8,384]{2,1,0:T(8,128)(2,1)} %get-tuple-element.13), channel_id=1, source_target_pairs={{32,64},{64,32},{96,128},{128,96},{160,192},{192,160},{33,65},{65,... | collective-permute-start | bytes 55304 | tf_op jit(solution)/shard_map/ppermute | solution.py:32
  3.7 0.9 %copy-start.1 = (bf16[2,8,8,384]{3,2,1,0:T(8,128)(2,1)S(1)}, bf16[2,8,8,384]{3,2,1,0:T(8,128)(2,1)}, u32[]{:S(2)}) copy-start(bf16[2,8,8,384]{3,2,1,0:T(8,128)(2,1)} %cache.5) | copy-start | bytes 294916
  4.6 0.8 %copy-start.4 = (bf16[8,8,384]{2,1,0:T(8,128)(2,1)S(1)}, bf16[8,8,384]{2,1,0:T(8,128)(2,1)}, u32[]{:S(2)}) copy-start(bf16[8,8,384]{2,1,0:T(8,128)(2,1)} %hidden.5) | copy-start | bytes 147460
  5.4 8.4 %slice-start = ((s8[7962624]{0:T(1024)(128)(4,1)}), s8[4194304]{0:T(1024)(128)(4,1)S(1)}, s32[]{:S(2)}) async-start(s8[7962624]{0:T(1024)(128)(4,1)} %bitcast.5), calls=%async_computation.2 | async-start | bytes 8388608
  5.5 8.3 %slice-start.1 = ((s8[7962624]{0:T(1024)(128)(4,1)}), s8[3768320]{0:T(1024)(128)(4,1)S(1)}, s32[]{:S(2)}) async-start(s8[7962624]{0:T(1024)(128)(4,1)} %bitcast.5), calls=%async_computation.3 | async-start | bytes 7536640
  5.5 8.3 %copy-start = (bf16[384,1152]{1,0:T(8,128)(2,1)S(1)}, bf16[384,1152]{1,0:T(8,128)(2,1)}, u32[]{:S(2)}) copy-start(bf16[384,1152]{1,0:T(8,128)(2,1)} %w_qkv.3) | copy-start | bytes 2654212
  5.5 8.3 %copy-start.2 = (bf16[2,8,8,384]{3,2,1,0:T(8,128)(2,1)S(1)}, bf16[2,8,8,384]{3,2,1,0:T(8,128)(2,1)}, u32[]{:S(2)}) copy-start(bf16[2,8,8,384]{3,2,1,0:T(8,128)(2,1)} %cache.5) | copy-start | bytes 294916
  5.5 8.3 %copy-start.5 = (bf16[8,8,384]{2,1,0:T(8,128)(2,1)S(1)}, bf16[8,8,384]{2,1,0:T(8,128)(2,1)}, u32[]{:S(2)}) copy-start(bf16[8,8,384]{2,1,0:T(8,128)(2,1)} %hidden.5) | copy-start | bytes 147460
  5.6 8.3 %copy-start.6 = (bf16[8,8,384]{2,1,0:T(8,128)(2,1)S(1)}, bf16[8,8,384]{2,1,0:T(8,128)(2,1)}, u32[]{:S(2)}) copy-start(bf16[8,8,384]{2,1,0:T(8,128)(2,1)} %param.12) | copy-start | bytes 147460
  5.6 8.3 %copy-start.7 = (f32[1152]{0:T(1024)S(1)}, f32[1152]{0:T(1024)}, u32[]{:S(2)}) copy-start(f32[1152]{0:T(1024)} %b_qkv.3) | copy-start | bytes 13828
  5.6 8.3 %copy-start.8 = (f32[384]{0:T(512)S(1)}, f32[384]{0:T(512)}, u32[]{:S(2)}) copy-start(f32[384]{0:T(512)} %norm_gain.1) | copy-start | bytes 4612
  5.6 8.3 %copy-start.9 = (f32[384]{0:T(512)S(1)}, f32[384]{0:T(512)}, u32[]{:S(2)}) copy-start(f32[384]{0:T(512)} %conv_bias.1) | copy-start | bytes 4612
  5.6 8.3 %copy-start.10 = (f32[384]{0:T(512)S(1)}, f32[384]{0:T(512)}, u32[]{:S(2)}) copy-start(f32[384]{0:T(512)} %attn_gain.1) | copy-start | bytes 4612
  5.7 4.9 %collective-permute-start.2 = (bf16[3,10,384]{2,1,0:T(8,128)(2,1)S(1)}, bf16[3,10,384]{2,1,0:T(8,128)(2,1)S(1)}, u32[]{:S(2)}, u32[]{:S(2)}) collective-permute-start(bf16[3,10,384]{2,1,0:T(8,128)(2,1)S(1)} %get-tuple-element.14), channel_id=1, source_target_pairs={{0,1},{1,0},{2,3},{3,2},{4,5},{5,4},{6,7},{7,6},{8,9},{9,8},{10,11... | collective-permute-start | bytes 69128 | tf_op jit(solution)/shard_map/ppermute | solution.py:32
  5.8 8.0 %collective-permute-start.3 = (bf16[3,10,384]{2,1,0:T(8,128)(2,1)S(1)}, bf16[3,10,384]{2,1,0:T(8,128)(2,1)S(1)}, u32[]{:S(2)}, u32[]{:S(2)}) collective-permute-start(bf16[3,10,384]{2,1,0:T(8,128)(2,1)S(1)} %get-tuple-element.15), channel_id=1, source_target_pairs={{1,2},{2,1},{3,4},{4,3},{5,6},{6,5},{7,8},{8,7},{9,10},{10,9},{11,... | collective-permute-start | bytes 69128 | tf_op jit(solution)/shard_map/ppermute | solution.py:32
  16.5 16.1 %collective-permute-start.4 = (bf16[64,384]{1,0:T(8,128)(2,1)S(1)}, bf16[64,384]{1,0:T(8,128)(2,1)S(1)}, u32[]{:S(2)}, u32[]{:S(2)}) collective-permute-start(bf16[64,384]{1,0:T(8,128)(2,1)S(1)} %get-tuple-element.17.own), channel_id=1, source_target_pairs={{0,16},{4,20},{8,24},{12,28},{16,0},{20,4},{24,8},{28,12},{1,17},{... | collective-permute-start | bytes 147464 | tf_op jit(solution)/shard_map/ppermute | solution.py:310
  22.8 26.2 %all-to-all-start = ((bf16[16,64,384]{2,1,0:T(8,128)(2,1)}), bf16[16,64,384]{2,1,0:T(8,128)(2,1)S(1)}, u32[]{:S(2)}, u32[]{:S(2)}) async-start(bf16[16,64,384]{2,1,0:T(8,128)(2,1)} %bitcast.2), calls=%async_computation | async-start | bytes 1572864 | tf_op jit(solution)/shard_map/all_to_all | solution.py:309
  32.6 38.3 %copy-start.3 = (bf16[384,384]{1,0:T(8,128)(2,1)S(1)}, bf16[384,384]{1,0:T(8,128)(2,1)}, u32[]{:S(2)}) copy-start(bf16[384,384]{1,0:T(8,128)(2,1)} %w_proj.1) | copy-start | bytes 884740
  32.6 38.3 %copy-start.11 = (f32[384]{0:T(512)S(1)}, f32[384]{0:T(512)}, u32[]{:S(2)}) copy-start(f32[384]{0:T(512)} %b_proj.1) | copy-start | bytes 4612
  32.7 5.6 %collective-permute-start.7 = (bf16[128,384]{1,0:T(8,128)(2,1)S(1)}, bf16[128,384]{1,0:T(8,128)(2,1)S(1)}, u32[]{:S(2)}, u32[]{:S(2)}) collective-permute-start(bf16[128,384]{1,0:T(8,128)(2,1)S(1)} %shard_map.113), channel_id=1, source_target_pairs={{0,28},{4,0},{8,4},{12,8},{16,12},{20,16},{24,20},{28,24},{1,29},{... | collective-permute-start | bytes 294920 | tf_op jit(solution)/shard_map/ppermute | solution.py:311
  33.8 5.6 %collective-permute-start.6 = (bf16[128,384]{1,0:T(8,128)(2,1)S(1)}, bf16[128,384]{1,0:T(8,128)(2,1)S(1)}, u32[]{:S(2)}, u32[]{:S(2)}) collective-permute-start(bf16[128,384]{1,0:T(8,128)(2,1)S(1)} %shard_map.113), channel_id=1, source_target_pairs={{0,4},{4,8},{8,12},{12,16},{16,20},{20,24},{24,28},{28,0},{1,5},{5... | collective-permute-start | bytes 294920 | tf_op jit(solution)/shard_map/ppermute | solution.py:311
  34.8 6.9 %collective-permute-start.5 = (bf16[128,384]{1,0:T(8,128)(2,1)S(1)}, bf16[128,384]{1,0:T(8,128)(2,1)S(1)}, u32[]{:S(2)}, u32[]{:S(2)}) collective-permute-start(bf16[128,384]{1,0:T(8,128)(2,1)S(1)} %shard_map.113), channel_id=1, source_target_pairs={{0,8},{4,12},{8,0},{12,4},{16,24},{20,28},{24,16},{28,20},{1,9},{5... | collective-permute-start | bytes 294920 | tf_op jit(solution)/shard_map/ppermute | solution.py:311
  41.7 1.8 %collective-permute-start.8 = (bf16[512,384]{1,0:T(8,128)(2,1)S(1)}, bf16[512,384]{1,0:T(8,128)(2,1)S(1)}, u32[]{:S(2)}, u32[]{:S(2)}) collective-permute-start(bf16[512,384]{1,0:T(8,128)(2,1)S(1)} %pad_maximum_fusion.line), channel_id=1, source_target_pairs={{0,1},{1,0},{2,3},{3,2},{4,5},{5,4},{6,7},{7,6},{8,9},{9,8},{10,11... | collective-permute-start | bytes 1179656 | tf_op jit(solution)/shard_map/ppermute | solution.py:312

commit v2 on v1

--- a/solution.py
+++ b/solution.py
@@ -10,7 +10,7 @@
 
 ROW = ("x", "ylo")
 COL = ("z", "yhi", "core")
-PLANE = ("x", "ylo", "yhi")
+PLANE = ("x", "yhi", "ylo")
 C = 384
 TILE = 8
 PIX = TILE * TILE
@@ -24,12 +24,15 @@
 
 def pairs(count):
     inner = [(i, i ^ 1) for i in range(count)]
-    outer = [(i, ((i + 1) ^ 1) - 1) for i in range(1, count - 1)]
+    outer = [(i, (((i + 1) ^ 1) - 1) % count) for i in range(count)]
     return inner, outer
 
 
 def swapped(edges, axes):
-    return [lax.ppermute(edge, axes, links) for edge, links in zip(edges, pairs(lax.axis_size(axes)))]
+    inner, outer = pairs(lax.axis_size(axes))
+    far = lax.ppermute(edges[1], axes, outer)
+    near = lax.ppermute(edges[0], axes, inner)
+    return near, far
 
 
 HBM = pl.BlockSpec(memory_space=pltpu.HBM)
@@ -50,6 +53,16 @@
         copy.wait()
 
 
+def inside_rows(edge):
+    place = 2 * lax.axis_index("x") + lax.axis_index("ylo")
+    return jnp.where((place == 0) | (place == 7), jnp.zeros_like(edge), edge)
+
+
+def inside_cols(edge):
+    place = 4 * lax.axis_index("z") + 2 * lax.axis_index("yhi") + lax.axis_index("core")
+    return jnp.where((place == 0) | (place == 31), jnp.zeros_like(edge), edge)
+
+
 def row_kernel(cache, hidden, inner, outer, sems):
     odd = lax.axis_index("ylo")
     moves = []
@@ -88,12 +101,12 @@
     )(cache, hidden)
 
 
-def column_kernel(sides, row_inner, row_outer, inner, outer):
+def column_kernel(sides, row_outer, row_inner, inner, outer):
     row_odd = lax.axis_index("ylo")
     odd = lax.axis_index("core")
     for frame in range(3):
         from_inner = row_inner[frame].astype(F32)
-        from_outer = row_outer[frame].astype(F32)
+        from_outer = inside_rows(row_outer[frame].astype(F32))
         above = jnp.where(row_odd == 1, from_inner, from_outer)
         below = jnp.where(row_odd == 1, from_outer, from_inner)
         left, right = [
@@ -113,7 +126,7 @@
         out_shape=[edge, edge],
         compiler_params=pltpu.CompilerParams(vmem_limit_bytes=4 << 20),
         cost_estimate=pl.CostEstimate(flops=1 << 34, bytes_accessed=1 << 20, transcendentals=0),
-    )(sides, row_inner, row_outer)
+    )(sides, row_outer, row_inner)
 
 
 def rms(floats, gain):
@@ -121,7 +134,7 @@
 
 
 def conv_kernel(
-    cache, hidden, row_inner, row_outer, col_inner, col_outer, weight, skip,
+    cache, hidden, row_outer, row_inner, col_outer, col_inner, weight, skip,
     norm_gain, conv_bias, attn_gain, w_qkv, b_qkv, middle, normed, queries, wide, shifted,
 ):
     row_odd = lax.axis_index("ylo")
@@ -131,9 +144,9 @@
         own = cache[frame] if frame < 2 else hidden[...]
         wide[pl.ds(1, TILE), 1 : 1 + TILE] = own.astype(F32)
         wide[9 - 9 * row_odd, 1 : 1 + TILE] = row_inner[frame].astype(F32)
-        wide[9 * row_odd, 1 : 1 + TILE] = row_outer[frame].astype(F32)
+        wide[9 * row_odd, 1 : 1 + TILE] = inside_rows(row_outer[frame].astype(F32))
         from_inner = col_inner[frame].astype(F32)
-        from_outer = col_outer[frame].astype(F32)
+        from_outer = inside_cols(col_outer[frame].astype(F32))
         wide[:, 0] = jnp.where(odd == 1, from_inner, from_outer)
         wide[:, 1 + TILE] = jnp.where(odd == 1, from_outer, from_inner)
         block = wide[:, 0 : TILE + 2]
@@ -174,7 +187,7 @@
             pltpu.VMEM((3, 3, TILE + 2, TILE, C), F32),
         ],
         compiler_params=pltpu.CompilerParams(vmem_limit_bytes=24 << 20),
-    )(cache, hidden, *rows, *cols, weight, skip, norm_gain, conv_bias, attn_gain, w_qkv, b_qkv)
+    )(cache, hidden, *rows[::-1], *cols[::-1], weight, skip, norm_gain, conv_bias, attn_gain, w_qkv, b_qkv)
 
 
 def pair_kernel(own, far, both):
@@ -189,6 +202,10 @@
         compiler_params=pltpu.CompilerParams(vmem_limit_bytes=4 << 20),
         cost_estimate=pl.CostEstimate(flops=1 << 34, bytes_accessed=1 << 20, transcendentals=0),
     )(own, far)
+
+
+def estimate(flops):
+    return pl.CostEstimate(flops=flops, bytes_accessed=1 << 20, transcendentals=0)
 
 
 def split3(value):
@@ -199,25 +216,47 @@
     return first.astype(F32), second.astype(F32), third.astype(F32)
 
 
-def attend_kernel(queries, line, other, w_qkv, b_qkv, partial):
-    normed = jnp.concatenate([line[...], other[...]], axis=0)
-    projected = jnp.dot(normed, w_qkv[:, C:], preferred_element_type=F32) + b_qkv[C:]
-    key_block = projected[:, :C].astype(BF16)
-    values = projected[:, C:].astype(BF16).T
-    scores = lax.dot_general(
-        key_block, queries[...], (((1,), (1,)), ((), ())), preferred_element_type=F32
-    ) * (math.log2(math.e) / math.sqrt(C))
-    top = jnp.max(scores, axis=0, keepdims=True)
-    weights = jnp.exp2(scores - top)
-    denom = jnp.sum(weights, axis=0, keepdims=True)
-    weights = weights.astype(BF16)
+def project_kernel(normed, w_qkv, b_qkv, key_block, values):
+    projected = jnp.dot(normed[...], w_qkv[:, C:], preferred_element_type=F32) + b_qkv[C:]
+    key_block[...] = projected[:, :C].astype(BF16)
+    values[...] = projected[:, C:].astype(BF16).T
+
+
+def project_stage(normed, w_qkv, b_qkv):
+    count = normed.shape[0]
+    return pl.pallas_call(
+        project_kernel,
+        out_shape=[
+            jax.ShapeDtypeStruct((count, C), BF16),
+            jax.ShapeDtypeStruct((C, count), BF16),
+        ],
+        compiler_params=pltpu.CompilerParams(vmem_limit_bytes=16 << 20),
+        cost_estimate=estimate(1 << 30),
+    )(normed, w_qkv, b_qkv)
+
+
+def attend_kernel(queries, line_keys, line_values, other, w_qkv, b_qkv, partial):
+    projected = jnp.dot(other[...], w_qkv[:, C:], preferred_element_type=F32) + b_qkv[C:]
+    other_keys = projected[:, :C].astype(BF16)
+    other_values = projected[:, C:].astype(BF16).T
+    scores = [
+        lax.dot_general(
+            keys[...], queries[...], (((1,), (1,)), ((), ())), preferred_element_type=F32
+        )
+        * (math.log2(math.e) / math.sqrt(C))
+        for keys in (line_keys, other_keys)
+    ]
+    top = jnp.maximum(*[jnp.max(part, axis=0, keepdims=True) for part in scores])
+    weights = [jnp.exp2(part - top) for part in scores]
+    denom = sum(jnp.sum(part, axis=0, keepdims=True) for part in weights)
+    weights = jnp.concatenate([part.astype(BF16) for part in weights], axis=0)
+    values = jnp.concatenate([line_values[...], other_values], axis=1)
     parts = split3(top) + split3(denom)
     stats = jnp.concatenate(parts + (jnp.zeros((2, QUERIES), F32),), axis=0)
     for place in range(SENDS):
         group = QUERIES // SENDS
-        numer = jnp.dot(
-            values, weights[:, place * group : (place + 1) * group], preferred_element_type=F32
-        ).T.astype(BF16)
+        span = slice(place * group, (place + 1) * group)
+        numer = jnp.dot(values, weights[:, span], preferred_element_type=F32).T.astype(BF16)
         first = place * group // PIX
         for index in range(group // PIX):
             low = (first + index) * PIX
@@ -234,8 +273,8 @@
     return pl.pallas_call(
         attend_kernel,
         out_shape=jax.ShapeDtypeStruct((16, 3 * PIX + 8, LANES), BF16),
-        compiler_params=pltpu.CompilerParams(vmem_limit_bytes=40 << 20),
-    )(queries, line, other, w_qkv, b_qkv)
+        compiler_params=pltpu.CompilerParams(vmem_limit_bytes=24 << 20),
+    )(queries, *line, other, w_qkv, b_qkv)
 
 
 def finish_kernel(partials, middle, w_proj, b_proj, block_out):
@@ -308,9 +347,15 @@
     )
     all_queries = lax.all_to_all(queries, PLANE, 0, 0, tiled=True)
     far = pair_stage(normed, lax.ppermute(normed, "z", flips(4)))
-    own_line = jnp.concatenate([far] + [lax.ppermute(far, "z", links) for links in (flips(2), steps(1), steps(-1))], axis=0)
+    own_line = jnp.concatenate([far] + [lax.ppermute(far, "z", links) for links in (steps(1), steps(-1), flips(2))], axis=0)
     other_line = lax.ppermute(own_line, "core", flips(1, 2))
-    partial = attend_stage(all_queries, own_line, other_line, w_qkv, b_qkv)
+    partial = attend_stage(
+        all_queries,
+        project_stage(own_line, w_qkv, b_qkv),
+        other_line,
+        w_qkv,
+        b_qkv,
+    )
     partials = lax.all_to_all(partial, PLANE, 0, 0, tiled=True)
     block_out = finish_stage(partials, middle, w_proj, b_proj)
     return block_out.reshape(TILE, TILE, C)

time: 72.6 us -> 64.8 us (0.89)
  starting transfers between devices: 28.2 us -> 21 us
    all_to_all x1, starting transfers between devices: 9.77 us -> 4.19 us  [shards(): all_queries = lax.all_to_all(queries, PLANE, 0, 0, tiled=True)]
    all_to_all x1, waiting for transfers between devices: 5.52 us -> 3.38 us  [shards(): all_queries = lax.all_to_all(queries, PLANE, 0, 0, tiled=True)]
    ppermute x4, waiting for transfers between devices: 3.22 us -> 4.84 us  [the longest x2 3.18 us: swapped(): far = lax.ppermute(edges[1], axes, outer)]
    ppermute x3, starting transfers between devices: 4.79 us -> 3.43 us  [shards(): lax.ppermute(far, 'z', links)]
  transfers between devices with their start and end apart: 10 -> 10, of which waited for: 6 -> 7; matrix products, arithmetic and copies ran while one was open for 0% -> 0% of each run, Pallas kernels for 0% -> 1%
where the time goes in v2:
time: 64.8 us; the launch traced here: 64.5 us
  starting transfers between devices  21 us (32%)
  blocking collectives  18.1 us (28%)
  waiting for transfers between devices  14.2 us (22%)
  Pallas kernels  9.18 us (14%)
  local copies, waits for them, and re-layouts  1.77 us (3%)
    all_to_all x1, blocking collectives, shards(): partials = lax.all_to_all(partial, PLANE, 0, 0, tiled=True)  18.1 us
    ppermute x1, starting transfers between devices, shards(): far = pair_stage(normed, lax.ppermute(normed, 'z', flips(4)))  6.29 us
    ppermute x3, waiting for transfers between devices, shards(): lax.ppermute(far, 'z', links)  4.9 us
    ppermute x2, starting transfers between devices, swapped(): far = lax.ppermute(edges[1], axes, outer)  4.74 us
    all_to_all x1, starting transfers between devices, shards(): all_queries = lax.all_to_all(queries, PLANE, 0, 0, tiled=True)  4.19 us
    ppermute x3, starting transfers between devices, shards(): lax.ppermute(far, 'z', links)  3.43 us
    all_to_all x1, waiting for transfers between devices, shards(): all_queries = lax.all_to_all(queries, PLANE, 0, 0, tiled=True)  3.38 us
    ppermute x2, waiting for transfers between devices, swapped(): far = lax.ppermute(edges[1], axes, outer)  3.18 us
  transfers between devices with their start and end apart: 10, of which 7 were waited for; matrix products, arithmetic and copies ran while one was open for 0% of the time, Pallas kernels for 1%

profile of v2, /device:TPU:32, one launch (start us, length us, event | category | flops | bytes accessed | tf_op | source)
XLA Modules:
  0.0 64.5 jit_solution(16464375106027178122)
XLA Ops:
  0.0 1.4 %shard_map.109 = (bf16[3,8,384]{2,1,0:T(8,128)(2,1)}, bf16[3,8,384]{2,1,0:T(8,128)(2,1)}) custom-call(bf16[2,8,8,384]{3,2,1,0:T(8,128)(2,1)} %cache.5, bf16[8,8,384]{2,1,0:T(8,128)(2,1)} %hidden.5), custom_call_target="tpu_custom_call" | custom-call | tf_op jit(solution)/shard_map/pallas_call | solution.py:77
  1.4 3.9 %collective-permute-start = (bf16[3,8,384]{2,1,0:T(8,128)(2,1)}, bf16[3,8,384]{2,1,0:T(8,128)(2,1)S(1)}, u32[]{:S(2)}, u32[]{:S(2)}) collective-permute-start(bf16[3,8,384]{2,1,0:T(8,128)(2,1)} %get-tuple-element.14), channel_id=1, source_target_pairs={{0,224},{32,64},{64,32},{96,128},{128,96},{160,192},{192,160},{224... | collective-permute-start | bytes 55304 | tf_op jit(solution)/shard_map/ppermute | solution.py:33
  5.3 0.9 %copy-done.1 = bf16[2,8,8,384]{3,2,1,0:T(8,128)(2,1)S(1)} copy-done((bf16[2,8,8,384]{3,2,1,0:T(8,128)(2,1)S(1)}, bf16[2,8,8,384]{3,2,1,0:T(8,128)(2,1)}, u32[]{:S(2)}) %copy-start.1) | copy-done | bytes 98328
  6.2 0.8 %copy-done.4 = bf16[8,8,384]{2,1,0:T(8,128)(2,1)S(1)} copy-done((bf16[8,8,384]{2,1,0:T(8,128)(2,1)S(1)}, bf16[8,8,384]{2,1,0:T(8,128)(2,1)}, u32[]{:S(2)}) %copy-start.4) | copy-done | bytes 49176
  7.0 0.1 shard_map.110.sides
  7.0 0.0 slice-start.1
  7.1 0.0 copy-start
  7.1 0.0 copy-start.2
  7.1 0.0 copy-start.5
  7.1 0.0 copy-start.6
  7.1 0.0 copy-start.7
  7.1 0.0 copy-start.10
  7.2 0.4 collective-permute-done.row_outer
  7.6 1.7 %collective-permute-done.1.row_inner = bf16[3,8,384]{2,1,0:T(8,128)(2,1)S(1)} collective-permute-done((bf16[3,8,384]{2,1,0:T(8,128)(2,1)}, bf16[3,8,384]{2,1,0:T(8,128)(2,1)S(1)}, u32[]{:S(2)}, u32[]{:S(2)}) %collective-permute-start.1) | collective-permute-done | bytes 18464 | tf_op jit(solution)/shard_map/ppermute | solution.py:34
  9.3 0.9 %collective-permute-start.2 = (bf16[3,10,384]{2,1,0:T(8,128)(2,1)S(1)}, bf16[3,10,384]{2,1,0:T(8,128)(2,1)S(1)}, u32[]{:S(2)}, u32[]{:S(2)}) collective-permute-start(bf16[3,10,384]{2,1,0:T(8,128)(2,1)S(1)} %get-tuple-element.16), channel_id=1, source_target_pairs={{0,31},{1,2},{2,1},{3,4},{4,3},{5,6},{6,5},{7,8},{8,7},{9,10},{10,... | collective-permute-start | bytes 69128 | tf_op jit(solution)/shard_map/ppermute | solution.py:33
  10.2 2.2 %collective-permute-start.3 = (bf16[3,10,384]{2,1,0:T(8,128)(2,1)S(1)}, bf16[3,10,384]{2,1,0:T(8,128)(2,1)S(1)}, u32[]{:S(2)}, u32[]{:S(2)}) collective-permute-start(bf16[3,10,384]{2,1,0:T(8,128)(2,1)S(1)} %get-tuple-element.17), channel_id=1, source_target_pairs={{0,1},{1,0},{2,3},{3,2},{4,5},{5,4},{6,7},{7,6},{8,9},{9,8},{10,11... | collective-permute-start | bytes 69128 | tf_op jit(solution)/shard_map/ppermute | solution.py:34
  12.4 2.8 %collective-permute-done.2.col_outer = bf16[3,10,384]{2,1,0:T(8,128)(2,1)S(1)} collective-permute-done((bf16[3,10,384]{2,1,0:T(8,128)(2,1)S(1)}, bf16[3,10,384]{2,1,0:T(8,128)(2,1)S(1)}, u32[]{:S(2)}, u32[]{:S(2)}) %collective-permute-start.2) | collective-permute-done | bytes 23072 | tf_op jit(solution)/shard_map/ppermute | solution.py:33
  15.2 2.6 %shard_map.112 = (bf16[64,384]{1,0:T(8,128)(2,1)S(1)}, bf16[64,384]{1,0:T(8,128)(2,1)S(1)}, bf16[1024,384]{1,0:T(8,128)(2,1)}) custom-call(bf16[2,8,8,384]{3,2,1,0:T(8,128)(2,1)S(1)} %copy-done.2, bf16[8,8,384]{2,1,0:T(8,128)(2,1)S(1)} %copy-done.5, bf16[3,8,384]{2,1,0:T(8,128)(2,1)S(1)} %collective-permute-done.row_outer, ...), custom_call_target="tpu_custom_call" | custom-call | tf_op jit(solution)/shard_map/pallas_call | solution.py:182
  17.9 6.3 %collective-permute-start.4 = (bf16[64,384]{1,0:T(8,128)(2,1)S(1)}, bf16[64,384]{1,0:T(8,128)(2,1)S(1)}, u32[]{:S(2)}, u32[]{:S(2)}) collective-permute-start(bf16[64,384]{1,0:T(8,128)(2,1)S(1)} %get-tuple-element.19.own), channel_id=1, source_target_pairs={{0,16},{4,20},{8,24},{12,28},{16,0},{20,4},{24,8},{28,12},{1,17},{... | collective-permute-start | bytes 147464 | tf_op jit(solution)/shard_map/ppermute | solution.py:349
  24.2 4.2 %all-to-all-start = ((bf16[16,64,384]{2,1,0:T(8,128)(2,1)}), bf16[16,64,384]{2,1,0:T(8,128)(2,1)S(1)}, u32[]{:S(2)}, u32[]{:S(2)}) async-start(bf16[16,64,384]{2,1,0:T(8,128)(2,1)} %bitcast.2), calls=%async_computation | async-start | bytes 1572864 | tf_op jit(solution)/shard_map/all_to_all | solution.py:348
  28.4 1.4 %collective-permute-start.7 = (bf16[128,384]{1,0:T(8,128)(2,1)S(1)}, bf16[128,384]{1,0:T(8,128)(2,1)S(1)}, u32[]{:S(2)}, u32[]{:S(2)}) collective-permute-start(bf16[128,384]{1,0:T(8,128)(2,1)S(1)} %shard_map.113), channel_id=1, source_target_pairs={{0,8},{4,12},{8,0},{12,4},{16,24},{20,28},{24,16},{28,20},{1,9},{5... | collective-permute-start | bytes 294920 | tf_op jit(solution)/shard_map/ppermute | solution.py:350
  29.8 1.2 %collective-permute-start.6 = (bf16[128,384]{1,0:T(8,128)(2,1)S(1)}, bf16[128,384]{1,0:T(8,128)(2,1)S(1)}, u32[]{:S(2)}, u32[]{:S(2)}) collective-permute-start(bf16[128,384]{1,0:T(8,128)(2,1)S(1)} %shard_map.113), channel_id=1, source_target_pairs={{0,28},{4,0},{8,4},{12,8},{16,12},{20,16},{24,20},{28,24},{1,29},{... | collective-permute-start | bytes 294920 | tf_op jit(solution)/shard_map/ppermute | solution.py:350
  31.0 0.9 %collective-permute-start.5 = (bf16[128,384]{1,0:T(8,128)(2,1)S(1)}, bf16[128,384]{1,0:T(8,128)(2,1)S(1)}, u32[]{:S(2)}, u32[]{:S(2)}) collective-permute-start(bf16[128,384]{1,0:T(8,128)(2,1)S(1)} %shard_map.113), channel_id=1, source_target_pairs={{0,4},{4,8},{8,12},{12,16},{16,20},{20,24},{24,28},{28,0},{1,5},{5... | collective-permute-start | bytes 294920 | tf_op jit(solution)/shard_map/ppermute | solution.py:350
  31.9 2.4 %collective-permute-done.7 = bf16[128,384]{1,0:T(8,128)(2,1)S(1)} collective-permute-done((bf16[128,384]{1,0:T(8,128)(2,1)S(1)}, bf16[128,384]{1,0:T(8,128)(2,1)S(1)}, u32[]{:S(2)}, u32[]{:S(2)}) %collective-permute-start.7) | collective-permute-done | bytes 98336 | tf_op jit(solution)/shard_map/ppermute | solution.py:350
  34.2 2.5 %collective-permute-done.6 = bf16[128,384]{1,0:T(8,128)(2,1)S(1)} collective-permute-done((bf16[128,384]{1,0:T(8,128)(2,1)S(1)}, bf16[128,384]{1,0:T(8,128)(2,1)S(1)}, u32[]{:S(2)}, u32[]{:S(2)}) %collective-permute-start.6) | collective-permute-done | bytes 98336 | tf_op jit(solution)/shard_map/ppermute | solution.py:350
  36.8 0.1 collective-permute-start.8
  36.9 0.6 shard_map.114
  37.6 1.1 %collective-permute-done.8.other = bf16[512,384]{1,0:T(8,128)(2,1)S(1)} collective-permute-done((bf16[512,384]{1,0:T(8,128)(2,1)S(1)}, bf16[512,384]{1,0:T(8,128)(2,1)S(1)}, u32[]{:S(2)}, u32[]{:S(2)}) %collective-permute-start.8) | collective-permute-done | bytes 393248 | tf_op jit(solution)/shard_map/ppermute | solution.py:351
  38.6 3.4 %all-to-all-done = bf16[16,64,384]{2,1,0:T(8,128)(2,1)S(1)} async-done(((bf16[16,64,384]{2,1,0:T(8,128)(2,1)}), bf16[16,64,384]{2,1,0:T(8,128)(2,1)S(1)}, u32[]{:S(2)}, u32[]{:S(2)}) %all-to-all-start) | async-done | bytes 786464 | tf_op jit(solution)/shard_map/all_to_all | solution.py:348
  42.0 3.2 %shard_map.115 = bf16[16,200,128]{2,1,0:T(8,128)(2,1)S(1)} custom-call(bf16[1024,384]{1,0:T(8,128)(2,1)S(1)} %bitcast.8, bf16[512,384]{1,0:T(8,128)(2,1)S(1)} %get-tuple-element.20.line_keys, bf16[384,512]{1,0:T(8,128)(2,1)S(1)} %get-tuple-element.21.line_values, bf16[512,384]{1,0:T(8,128)(2,1)S(1)} %collective-permute-done.8.other, ...), custom_call_target="tpu_custom_call" | custom-call | tf_op jit(solution)/shard_map/pallas_call | solution.py:273
  45.2 18.1 %all_to_all.16.partials = bf16[16,200,128]{2,1,0:T(8,128)(2,1)S(1)} all-to-all(bf16[16,200,128]{2,1,0:T(8,128)(2,1)S(1)} %shard_map.115), channel_id=1, replica_groups=mesh['x'=4,'ylo'=2,'z'=8,'yhi'=2,'core'=2] {'x','yhi','ylo'}, dimensions={0} | all-to-all | bytes 1638400 | tf_op jit(solution)/shard_map/all_to_all | solution.py:359
  63.3 1.2 %shard_map.116 = bf16[64,384]{1,0:T(8,128)(2,1)} custom-call(bf16[16,200,128]{2,1,0:T(8,128)(2,1)S(1)} %all_to_all.16.partials, bf16[64,384]{1,0:T(8,128)(2,1)S(1)} %get-tuple-element.22.middle, bf16[384,384]{1,0:T(8,128)(2,1)S(1)} %copy-done.3, f32[384]{0:T(512)S(1)} %copy-done.11), custom_call_target="tpu_custom_call" | custom-call | tf_op jit(solution)/shard_map/pallas_call | solution.py:305
  (27 shorter events, 0.1 us)
Async XLA Ops:
  1.4 6.2 %collective-permute-start = (bf16[3,8,384]{2,1,0:T(8,128)(2,1)}, bf16[3,8,384]{2,1,0:T(8,128)(2,1)S(1)}, u32[]{:S(2)}, u32[]{:S(2)}) collective-permute-start(bf16[3,8,384]{2,1,0:T(8,128)(2,1)} %get-tuple-element.14), channel_id=1, source_target_pairs={{0,224},{32,64},{64,32},{96,128},{128,96},{160,192},{192,160},{224... | collective-permute-start | bytes 55304 | tf_op jit(solution)/shard_map/ppermute | solution.py:33
  5.3 4.0 %collective-permute-start.1 = (bf16[3,8,384]{2,1,0:T(8,128)(2,1)}, bf16[3,8,384]{2,1,0:T(8,128)(2,1)S(1)}, u32[]{:S(2)}, u32[]{:S(2)}) collective-permute-start(bf16[3,8,384]{2,1,0:T(8,128)(2,1)} %get-tuple-element.15), channel_id=1, source_target_pairs={{0,32},{32,0},{64,96},{96,64},{128,160},{160,128},{192,224},{224,1... | collective-permute-start | bytes 55304 | tf_op jit(solution)/shard_map/ppermute | solution.py:34
  5.3 0.9 %copy-start.1 = (bf16[2,8,8,384]{3,2,1,0:T(8,128)(2,1)S(1)}, bf16[2,8,8,384]{3,2,1,0:T(8,128)(2,1)}, u32[]{:S(2)}) copy-start(bf16[2,8,8,384]{3,2,1,0:T(8,128)(2,1)} %cache.5) | copy-start | bytes 294916
  6.1 0.8 %copy-start.4 = (bf16[8,8,384]{2,1,0:T(8,128)(2,1)S(1)}, bf16[8,8,384]{2,1,0:T(8,128)(2,1)}, u32[]{:S(2)}) copy-start(bf16[8,8,384]{2,1,0:T(8,128)(2,1)} %hidden.5) | copy-start | bytes 147460
  6.9 8.2 %slice-start = ((s8[7962624]{0:T(1024)(128)(4,1)}), s8[4194304]{0:T(1024)(128)(4,1)S(1)}, s32[]{:S(2)}) async-start(s8[7962624]{0:T(1024)(128)(4,1)} %bitcast.5), calls=%async_computation.2 | async-start | bytes 8388608
  7.0 8.1 %slice-start.1 = ((s8[7962624]{0:T(1024)(128)(4,1)}), s8[3768320]{0:T(1024)(128)(4,1)S(1)}, s32[]{:S(2)}) async-start(s8[7962624]{0:T(1024)(128)(4,1)} %bitcast.5), calls=%async_computation.3 | async-start | bytes 7536640
  7.1 8.1 %copy-start = (bf16[384,1152]{1,0:T(8,128)(2,1)S(1)}, bf16[384,1152]{1,0:T(8,128)(2,1)}, u32[]{:S(2)}) copy-start(bf16[384,1152]{1,0:T(8,128)(2,1)} %w_qkv.5) | copy-start | bytes 2654212
  7.1 8.1 %copy-start.2 = (bf16[2,8,8,384]{3,2,1,0:T(8,128)(2,1)S(1)}, bf16[2,8,8,384]{3,2,1,0:T(8,128)(2,1)}, u32[]{:S(2)}) copy-start(bf16[2,8,8,384]{3,2,1,0:T(8,128)(2,1)} %cache.5) | copy-start | bytes 294916
  7.1 8.1 %copy-start.5 = (bf16[8,8,384]{2,1,0:T(8,128)(2,1)S(1)}, bf16[8,8,384]{2,1,0:T(8,128)(2,1)}, u32[]{:S(2)}) copy-start(bf16[8,8,384]{2,1,0:T(8,128)(2,1)} %hidden.5) | copy-start | bytes 147460
  7.1 8.1 %copy-start.6 = (bf16[8,8,384]{2,1,0:T(8,128)(2,1)S(1)}, bf16[8,8,384]{2,1,0:T(8,128)(2,1)}, u32[]{:S(2)}) copy-start(bf16[8,8,384]{2,1,0:T(8,128)(2,1)} %param.12) | copy-start | bytes 147460
  7.1 8.1 %copy-start.7 = (f32[1152]{0:T(1024)S(1)}, f32[1152]{0:T(1024)}, u32[]{:S(2)}) copy-start(f32[1152]{0:T(1024)} %b_qkv.5) | copy-start | bytes 13828
  7.1 8.1 %copy-start.8 = (f32[384]{0:T(512)S(1)}, f32[384]{0:T(512)}, u32[]{:S(2)}) copy-start(f32[384]{0:T(512)} %norm_gain.1) | copy-start | bytes 4612
  7.1 8.1 %copy-start.9 = (f32[384]{0:T(512)S(1)}, f32[384]{0:T(512)}, u32[]{:S(2)}) copy-start(f32[384]{0:T(512)} %conv_bias.1) | copy-start | bytes 4612
  7.1 8.1 %copy-start.10 = (f32[384]{0:T(512)S(1)}, f32[384]{0:T(512)}, u32[]{:S(2)}) copy-start(f32[384]{0:T(512)} %attn_gain.1) | copy-start | bytes 4612
  9.3 5.9 %collective-permute-start.2 = (bf16[3,10,384]{2,1,0:T(8,128)(2,1)S(1)}, bf16[3,10,384]{2,1,0:T(8,128)(2,1)S(1)}, u32[]{:S(2)}, u32[]{:S(2)}) collective-permute-start(bf16[3,10,384]{2,1,0:T(8,128)(2,1)S(1)} %get-tuple-element.16), channel_id=1, source_target_pairs={{0,31},{1,2},{2,1},{3,4},{4,3},{5,6},{6,5},{7,8},{8,7},{9,10},{10,... | collective-permute-start | bytes 69128 | tf_op jit(solution)/shard_map/ppermute | solution.py:33
  10.2 5.0 %collective-permute-start.3 = (bf16[3,10,384]{2,1,0:T(8,128)(2,1)S(1)}, bf16[3,10,384]{2,1,0:T(8,128)(2,1)S(1)}, u32[]{:S(2)}, u32[]{:S(2)}) collective-permute-start(bf16[3,10,384]{2,1,0:T(8,128)(2,1)S(1)} %get-tuple-element.17), channel_id=1, source_target_pairs={{0,1},{1,0},{2,3},{3,2},{4,5},{5,4},{6,7},{7,6},{8,9},{9,8},{10,11... | collective-permute-start | bytes 69128 | tf_op jit(solution)/shard_map/ppermute | solution.py:34
  17.9 10.5 %collective-permute-start.4 = (bf16[64,384]{1,0:T(8,128)(2,1)S(1)}, bf16[64,384]{1,0:T(8,128)(2,1)S(1)}, u32[]{:S(2)}, u32[]{:S(2)}) collective-permute-start(bf16[64,384]{1,0:T(8,128)(2,1)S(1)} %get-tuple-element.19.own), channel_id=1, source_target_pairs={{0,16},{4,20},{8,24},{12,28},{16,0},{20,4},{24,8},{28,12},{1,17},{... | collective-permute-start | bytes 147464 | tf_op jit(solution)/shard_map/ppermute | solution.py:349
  24.2 17.8 %all-to-all-start = ((bf16[16,64,384]{2,1,0:T(8,128)(2,1)}), bf16[16,64,384]{2,1,0:T(8,128)(2,1)S(1)}, u32[]{:S(2)}, u32[]{:S(2)}) async-start(bf16[16,64,384]{2,1,0:T(8,128)(2,1)} %bitcast.2), calls=%async_computation | async-start | bytes 1572864 | tf_op jit(solution)/shard_map/all_to_all | solution.py:348
  28.4 34.9 %copy-start.3 = (bf16[384,384]{1,0:T(8,128)(2,1)S(1)}, bf16[384,384]{1,0:T(8,128)(2,1)}, u32[]{:S(2)}) copy-start(bf16[384,384]{1,0:T(8,128)(2,1)} %w_proj.1) | copy-start | bytes 884740
  28.4 34.8 %copy-start.11 = (f32[384]{0:T(512)S(1)}, f32[384]{0:T(512)}, u32[]{:S(2)}) copy-start(f32[384]{0:T(512)} %b_proj.1) | copy-start | bytes 4612
  28.4 5.8 %collective-permute-start.7 = (bf16[128,384]{1,0:T(8,128)(2,1)S(1)}, bf16[128,384]{1,0:T(8,128)(2,1)S(1)}, u32[]{:S(2)}, u32[]{:S(2)}) collective-permute-start(bf16[128,384]{1,0:T(8,128)(2,1)S(1)} %shard_map.113), channel_id=1, source_target_pairs={{0,8},{4,12},{8,0},{12,4},{16,24},{20,28},{24,16},{28,20},{1,9},{5... | collective-permute-start | bytes 294920 | tf_op jit(solution)/shard_map/ppermute | solution.py:350
  29.8 6.9 %collective-permute-start.6 = (bf16[128,384]{1,0:T(8,128)(2,1)S(1)}, bf16[128,384]{1,0:T(8,128)(2,1)S(1)}, u32[]{:S(2)}, u32[]{:S(2)}) collective-permute-start(bf16[128,384]{1,0:T(8,128)(2,1)S(1)} %shard_map.113), channel_id=1, source_target_pairs={{0,28},{4,0},{8,4},{12,8},{16,12},{20,16},{24,20},{28,24},{1,29},{... | collective-permute-start | bytes 294920 | tf_op jit(solution)/shard_map/ppermute | solution.py:350
  31.0 5.8 %collective-permute-start.5 = (bf16[128,384]{1,0:T(8,128)(2,1)S(1)}, bf16[128,384]{1,0:T(8,128)(2,1)S(1)}, u32[]{:S(2)}, u32[]{:S(2)}) collective-permute-start(bf16[128,384]{1,0:T(8,128)(2,1)S(1)} %shard_map.113), channel_id=1, source_target_pairs={{0,4},{4,8},{8,12},{12,16},{16,20},{20,24},{24,28},{28,0},{1,5},{5... | collective-permute-start | bytes 294920 | tf_op jit(solution)/shard_map/ppermute | solution.py:350
  36.8 1.8 %collective-permute-start.8 = (bf16[512,384]{1,0:T(8,128)(2,1)S(1)}, bf16[512,384]{1,0:T(8,128)(2,1)S(1)}, u32[]{:S(2)}, u32[]{:S(2)}) collective-permute-start(bf16[512,384]{1,0:T(8,128)(2,1)S(1)} %pad_maximum_fusion.normed), channel_id=1, source_target_pairs={{0,1},{1,0},{2,3},{3,2},{4,5},{5,4},{6,7},{7,6},{8,9},{9,8},{10,11... | collective-permute-start | bytes 1179656 | tf_op jit(solution)/shard_map/ppermute | solution.py:351

commit v3 on v2

--- a/solution.py
+++ b/solution.py
@@ -63,42 +63,33 @@
     return jnp.where((place == 0) | (place == 31), jnp.zeros_like(edge), edge)
 
 
-def row_kernel(cache, hidden, inner, outer, sems):
+def edge_kernel(cache_h, hidden_h, outer, inner, sides, cache, hidden, wide, sems):
     odd = lax.axis_index("ylo")
-    moves = []
-    for edge, row in ((inner, 7 - 7 * odd), (outer, 7 * odd)):
-        moves.append((cache.at[:, row], edge.at[pl.ds(0, 2)]))
-        moves.append((hidden.at[row], edge.at[2]))
-    arrive(fetch(moves, sems))
-
-
-def row_edges(cache, hidden):
+    arrive(fetch(((cache_h, cache), (hidden_h, hidden)), sems))
+    for frame in range(3):
+        own = (cache[frame] if frame < 2 else hidden[...]).astype(F32)
+        wide[...] = own
+        outer[frame] = jnp.where(odd == 1, own[TILE - 1], own[0]).astype(BF16)
+        inner[frame] = jnp.where(odd == 1, own[0], own[TILE - 1]).astype(BF16)
+        for place, col in enumerate((0, TILE - 1)):
+            sides[place, frame] = wide[:, col, :].astype(BF16)
+
+
+def own_edges(cache, hidden):
     edge = jax.ShapeDtypeStruct((3, TILE, C), BF16)
-    return pl.pallas_call(
-        row_kernel,
+    outer, inner, sides = pl.pallas_call(
+        edge_kernel,
         in_specs=[HBM, HBM],
-        out_shape=[edge, edge],
-        scratch_shapes=[pltpu.SemaphoreType.DMA((4,))],
-        compiler_params=pltpu.CompilerParams(vmem_limit_bytes=60 << 20),
+        out_shape=[edge, edge, jax.ShapeDtypeStruct((2, 3, TILE, C), BF16)],
+        scratch_shapes=[
+            pltpu.VMEM((2, TILE, TILE, C), BF16),
+            pltpu.VMEM((TILE, TILE, C), BF16),
+            pltpu.VMEM((TILE, TILE, C), F32),
+            pltpu.SemaphoreType.DMA((2,)),
+        ],
+        compiler_params=pltpu.CompilerParams(vmem_limit_bytes=55120 << 10),
     )(cache, hidden)
-
-
-def side_kernel(cache, hidden, sides, wide):
-    for frame in range(3):
-        own = cache[frame] if frame < 2 else hidden[...]
-        wide[frame] = own.astype(F32)
-        for place, col in enumerate((0, TILE - 1)):
-            sides[place, frame] = wide[frame, :, col, :].astype(BF16)
-
-
-def own_sides(cache, hidden):
-    return pl.pallas_call(
-        side_kernel,
-        out_shape=jax.ShapeDtypeStruct((2, 3, TILE, C), BF16),
-        scratch_shapes=[pltpu.VMEM((3, TILE, TILE, C), F32)],
-        compiler_params=pltpu.CompilerParams(vmem_limit_bytes=4 << 20),
-        cost_estimate=pl.CostEstimate(flops=1 << 31, bytes_accessed=1 << 20, transcendentals=0),
-    )(cache, hidden)
+    return (inner, outer), sides
 
 
 def column_kernel(sides, row_outer, row_inner, inner, outer):
@@ -330,8 +321,9 @@
     w_proj,
     b_proj,
 ):
-    rows = swapped(row_edges(cache_frames, hidden_in), ROW)
-    cols = swapped(column_edges(own_sides(cache_frames, hidden_in), *rows), COL)
+    edges, own_sides = own_edges(cache_frames, hidden_in)
+    rows = swapped(edges, ROW)
+    cols = swapped(column_edges(own_sides, *rows), COL)
     middle, normed, queries = conv_stage(
         cache_frames,
         hidden_in,

time: 64.8 us -> 64.2 us (level)
  local copies, waits for them, and re-layouts: 1.77 us -> 0.06 us
  waiting for transfers between devices: 14.2 us -> 15.9 us
    unnamed x28 -> x22, local copies, waits for them, and re-layouts: 1.77 us -> 0.06 us
    ppermute x2, waiting for transfers between devices: 3.18 us -> 4.87 us  [swapped(): far = lax.ppermute(edges[1], axes, outer)]
    pallas_call x2 -> x1, Pallas kernels: 1.48 us -> 1.01 us  [own_edges(): pl.pallas_call(edge_kernel, in_specs=[HBM, HBM], out_shape=[edge, edge, j...]
where the time goes in v3:
time: 64.2 us; the launch traced here: 63.9 us
  starting transfers between devices  21 us (33%)
  blocking collectives  18.1 us (28%)
  waiting for transfers between devices  15.9 us (25%)
  Pallas kernels  8.67 us (14%)
    all_to_all x1, blocking collectives, shards(): partials = lax.all_to_all(partial, PLANE, 0, 0, tiled=True)  18.1 us
    ppermute x1, starting transfers between devices, shards(): far = pair_stage(normed, lax.ppermute(normed, 'z', flips(4)))  6.29 us
    ppermute x3, waiting for transfers between devices, shards(): lax.ppermute(far, 'z', links)  4.9 us
    ppermute x2, waiting for transfers between devices, swapped(): far = lax.ppermute(edges[1], axes, outer)  4.87 us
    ppermute x2, starting transfers between devices, swapped(): far = lax.ppermute(edges[1], axes, outer)  4.74 us
    all_to_all x1, starting transfers between devices, shards(): all_queries = lax.all_to_all(queries, PLANE, 0, 0, tiled=True)  4.21 us
    ppermute x3, starting transfers between devices, shards(): lax.ppermute(far, 'z', links)  3.42 us
    all_to_all x1, waiting for transfers between devices, shards(): all_queries = lax.all_to_all(queries, PLANE, 0, 0, tiled=True)  3.38 us
  transfers between devices with their start and end apart: 10, of which 7 were waited for; matrix products, arithmetic and copies ran while one was open for 0% of the time, Pallas kernels for 1%

profile of v3, /device:TPU:32, one launch (start us, length us, event | category | flops | bytes accessed | tf_op | source)
XLA Modules:
  0.0 63.9 jit_solution(3244342878229647326)
XLA Ops:
  0.0 1.0 %shard_map.109 = (bf16[3,8,384]{2,1,0:T(8,128)(2,1)S(1)}, bf16[3,8,384]{2,1,0:T(8,128)(2,1)S(1)}, bf16[2,3,8,384]{3,2,1,0:T(8,128)(2,1)S(1)}) custom-call(bf16[2,8,8,384]{3,2,1,0:T(8,128)(2,1)} %cache.1, bf16[8,8,384]{2,1,0:T(8,128)(2,1)} %hidden.1), custom_call_target="tpu_custom_call" | custom-call | tf_op jit(solution)/shard_map/pallas_call | solution.py:80
  1.0 3.9 %collective-permute-start = (bf16[3,8,384]{2,1,0:T(8,128)(2,1)S(1)}, bf16[3,8,384]{2,1,0:T(8,128)(2,1)S(1)}, u32[]{:S(2)}, u32[]{:S(2)}) collective-permute-start(bf16[3,8,384]{2,1,0:T(8,128)(2,1)S(1)} %get-tuple-element.15), channel_id=1, source_target_pairs={{0,224},{32,64},{64,32},{96,128},{128,96},{160,192},{192,160},{224... | collective-permute-start | bytes 55304 | tf_op jit(solution)/shard_map/ppermute | solution.py:33
  4.9 0.0 collective-permute-start.1
  4.9 2.1 %collective-permute-done.row_outer = bf16[3,8,384]{2,1,0:T(8,128)(2,1)S(1)} collective-permute-done((bf16[3,8,384]{2,1,0:T(8,128)(2,1)S(1)}, bf16[3,8,384]{2,1,0:T(8,128)(2,1)S(1)}, u32[]{:S(2)}, u32[]{:S(2)}) %collective-permute-start) | collective-permute-done | bytes 18464 | tf_op jit(solution)/shard_map/ppermute | solution.py:33
  7.0 1.7 %collective-permute-done.1.row_inner = bf16[3,8,384]{2,1,0:T(8,128)(2,1)S(1)} collective-permute-done((bf16[3,8,384]{2,1,0:T(8,128)(2,1)S(1)}, bf16[3,8,384]{2,1,0:T(8,128)(2,1)S(1)}, u32[]{:S(2)}, u32[]{:S(2)}) %collective-permute-start.1) | collective-permute-done | bytes 18464 | tf_op jit(solution)/shard_map/ppermute | solution.py:34
  8.6 0.0 copy-start.5
  8.7 0.0 copy-start.6
  8.7 0.0 copy-start.7
  8.7 0.0 copy-start.8
  8.7 0.0 copy-start.9
  8.8 0.9 %collective-permute-start.2 = (bf16[3,10,384]{2,1,0:T(8,128)(2,1)S(1)}, bf16[3,10,384]{2,1,0:T(8,128)(2,1)S(1)}, u32[]{:S(2)}, u32[]{:S(2)}) collective-permute-start(bf16[3,10,384]{2,1,0:T(8,128)(2,1)S(1)} %get-tuple-element.18), channel_id=1, source_target_pairs={{0,31},{1,2},{2,1},{3,4},{4,3},{5,6},{6,5},{7,8},{8,7},{9,10},{10,... | collective-permute-start | bytes 69128 | tf_op jit(solution)/shard_map/ppermute | solution.py:33
  9.6 2.2 %collective-permute-start.3 = (bf16[3,10,384]{2,1,0:T(8,128)(2,1)S(1)}, bf16[3,10,384]{2,1,0:T(8,128)(2,1)S(1)}, u32[]{:S(2)}, u32[]{:S(2)}) collective-permute-start(bf16[3,10,384]{2,1,0:T(8,128)(2,1)S(1)} %get-tuple-element.19), channel_id=1, source_target_pairs={{0,1},{1,0},{2,3},{3,2},{4,5},{5,4},{6,7},{7,6},{8,9},{9,8},{10,11... | collective-permute-start | bytes 69128 | tf_op jit(solution)/shard_map/ppermute | solution.py:34
  11.9 2.8 %collective-permute-done.2.col_outer = bf16[3,10,384]{2,1,0:T(8,128)(2,1)S(1)} collective-permute-done((bf16[3,10,384]{2,1,0:T(8,128)(2,1)S(1)}, bf16[3,10,384]{2,1,0:T(8,128)(2,1)S(1)}, u32[]{:S(2)}, u32[]{:S(2)}) %collective-permute-start.2) | collective-permute-done | bytes 23072 | tf_op jit(solution)/shard_map/ppermute | solution.py:33
  14.6 0.0 collective-permute-done.3.col_inner
  14.7 2.6 %shard_map.111 = (bf16[64,384]{1,0:T(8,128)(2,1)S(1)}, bf16[64,384]{1,0:T(8,128)(2,1)S(1)}, bf16[1024,384]{1,0:T(8,128)(2,1)}) custom-call(bf16[2,8,8,384]{3,2,1,0:T(8,128)(2,1)S(1)} %copy-done.2, bf16[8,8,384]{2,1,0:T(8,128)(2,1)S(1)} %copy-done.4, bf16[3,8,384]{2,1,0:T(8,128)(2,1)S(1)} %collective-permute-done.row_outer, ...), custom_call_target="tpu_custom_call" | custom-call | tf_op jit(solution)/shard_map/pallas_call | solution.py:173
  17.3 6.3 %collective-permute-start.4 = (bf16[64,384]{1,0:T(8,128)(2,1)S(1)}, bf16[64,384]{1,0:T(8,128)(2,1)S(1)}, u32[]{:S(2)}, u32[]{:S(2)}) collective-permute-start(bf16[64,384]{1,0:T(8,128)(2,1)S(1)} %get-tuple-element.21.own), channel_id=1, source_target_pairs={{0,16},{4,20},{8,24},{12,28},{16,0},{20,4},{24,8},{28,12},{1,17},{... | collective-permute-start | bytes 147464 | tf_op jit(solution)/shard_map/ppermute | solution.py:341
  23.6 4.2 %all-to-all-start = ((bf16[16,64,384]{2,1,0:T(8,128)(2,1)}), bf16[16,64,384]{2,1,0:T(8,128)(2,1)S(1)}, u32[]{:S(2)}, u32[]{:S(2)}) async-start(bf16[16,64,384]{2,1,0:T(8,128)(2,1)} %bitcast.2), calls=%async_computation | async-start | bytes 1572864 | tf_op jit(solution)/shard_map/all_to_all | solution.py:340
  27.9 0.0 copy-start.3
  27.9 0.0 copy-start.10
  27.9 1.4 %collective-permute-start.7 = (bf16[128,384]{1,0:T(8,128)(2,1)S(1)}, bf16[128,384]{1,0:T(8,128)(2,1)S(1)}, u32[]{:S(2)}, u32[]{:S(2)}) collective-permute-start(bf16[128,384]{1,0:T(8,128)(2,1)S(1)} %shard_map.112), channel_id=1, source_target_pairs={{0,8},{4,12},{8,0},{12,4},{16,24},{20,28},{24,16},{28,20},{1,9},{5... | collective-permute-start | bytes 294920 | tf_op jit(solution)/shard_map/ppermute | solution.py:342
  29.3 1.2 %collective-permute-start.6 = (bf16[128,384]{1,0:T(8,128)(2,1)S(1)}, bf16[128,384]{1,0:T(8,128)(2,1)S(1)}, u32[]{:S(2)}, u32[]{:S(2)}) collective-permute-start(bf16[128,384]{1,0:T(8,128)(2,1)S(1)} %shard_map.112), channel_id=1, source_target_pairs={{0,28},{4,0},{8,4},{12,8},{16,12},{20,16},{24,20},{28,24},{1,29},{... | collective-permute-start | bytes 294920 | tf_op jit(solution)/shard_map/ppermute | solution.py:342
  30.5 0.9 %collective-permute-start.5 = (bf16[128,384]{1,0:T(8,128)(2,1)S(1)}, bf16[128,384]{1,0:T(8,128)(2,1)S(1)}, u32[]{:S(2)}, u32[]{:S(2)}) collective-permute-start(bf16[128,384]{1,0:T(8,128)(2,1)S(1)} %shard_map.112), channel_id=1, source_target_pairs={{0,4},{4,8},{8,12},{12,16},{16,20},{20,24},{24,28},{28,0},{1,5},{5... | collective-permute-start | bytes 294920 | tf_op jit(solution)/shard_map/ppermute | solution.py:342
  31.3 2.4 %collective-permute-done.7 = bf16[128,384]{1,0:T(8,128)(2,1)S(1)} collective-permute-done((bf16[128,384]{1,0:T(8,128)(2,1)S(1)}, bf16[128,384]{1,0:T(8,128)(2,1)S(1)}, u32[]{:S(2)}, u32[]{:S(2)}) %collective-permute-start.7) | collective-permute-done | bytes 98336 | tf_op jit(solution)/shard_map/ppermute | solution.py:342
  33.7 2.5 %collective-permute-done.6 = bf16[128,384]{1,0:T(8,128)(2,1)S(1)} collective-permute-done((bf16[128,384]{1,0:T(8,128)(2,1)S(1)}, bf16[128,384]{1,0:T(8,128)(2,1)S(1)}, u32[]{:S(2)}, u32[]{:S(2)}) %collective-permute-start.6) | collective-permute-done | bytes 98336 | tf_op jit(solution)/shard_map/ppermute | solution.py:342
  36.2 0.0 collective-permute-done.5
  36.3 0.1 collective-permute-start.8
  36.4 0.6 %shard_map.113 = (bf16[512,384]{1,0:T(8,128)(2,1)S(1)}, bf16[384,512]{1,0:T(8,128)(2,1)S(1)}) custom-call(bf16[512,384]{1,0:T(8,128)(2,1)S(1)} %pad_maximum_fusion.normed, bf16[384,1152]{1,0:T(8,128)(2,1)S(1)} %copy-done.1, f32[1152]{0:T(1024)S(1)} %copy-done.6), custom_call_target="tpu_custom_call" | custom-call | flops 1073741824 | bytes 1048576 | tf_op jit(solution)/shard_map/pallas_call | solution.py:218
  37.0 1.1 %collective-permute-done.8.other = bf16[512,384]{1,0:T(8,128)(2,1)S(1)} collective-permute-done((bf16[512,384]{1,0:T(8,128)(2,1)S(1)}, bf16[512,384]{1,0:T(8,128)(2,1)S(1)}, u32[]{:S(2)}, u32[]{:S(2)}) %collective-permute-start.8) | collective-permute-done | bytes 393248 | tf_op jit(solution)/shard_map/ppermute | solution.py:343
  38.1 3.4 %all-to-all-done = bf16[16,64,384]{2,1,0:T(8,128)(2,1)S(1)} async-done(((bf16[16,64,384]{2,1,0:T(8,128)(2,1)}), bf16[16,64,384]{2,1,0:T(8,128)(2,1)S(1)}, u32[]{:S(2)}, u32[]{:S(2)}) %all-to-all-start) | async-done | bytes 786464 | tf_op jit(solution)/shard_map/all_to_all | solution.py:340
  41.5 3.2 %shard_map.114 = bf16[16,200,128]{2,1,0:T(8,128)(2,1)S(1)} custom-call(bf16[1024,384]{1,0:T(8,128)(2,1)S(1)} %bitcast.6, bf16[512,384]{1,0:T(8,128)(2,1)S(1)} %get-tuple-element.22.line_keys, bf16[384,512]{1,0:T(8,128)(2,1)S(1)} %get-tuple-element.23.line_values, bf16[512,384]{1,0:T(8,128)(2,1)S(1)} %collective-permute-done.8.other, ...), custom_call_target="tpu_custom_call" | custom-call | tf_op jit(solution)/shard_map/pallas_call | solution.py:264
  44.6 18.1 %all_to_all.16.partials = bf16[16,200,128]{2,1,0:T(8,128)(2,1)S(1)} all-to-all(bf16[16,200,128]{2,1,0:T(8,128)(2,1)S(1)} %shard_map.114), channel_id=1, replica_groups=mesh['x'=4,'ylo'=2,'z'=8,'yhi'=2,'core'=2] {'x','yhi','ylo'}, dimensions={0} | all-to-all | bytes 1638400 | tf_op jit(solution)/shard_map/all_to_all | solution.py:351
  62.7 1.2 %shard_map.115 = bf16[64,384]{1,0:T(8,128)(2,1)} custom-call(bf16[16,200,128]{2,1,0:T(8,128)(2,1)S(1)} %all_to_all.16.partials, bf16[64,384]{1,0:T(8,128)(2,1)S(1)} %get-tuple-element.24.middle, bf16[384,384]{1,0:T(8,128)(2,1)S(1)} %copy-done.3, f32[384]{0:T(512)S(1)} %copy-done.10), custom_call_target="tpu_custom_call" | custom-call | tf_op jit(solution)/shard_map/pallas_call | solution.py:296
  (19 shorter events, 0.1 us)
Async XLA Ops:
  1.0 6.0 %collective-permute-start = (bf16[3,8,384]{2,1,0:T(8,128)(2,1)S(1)}, bf16[3,8,384]{2,1,0:T(8,128)(2,1)S(1)}, u32[]{:S(2)}, u32[]{:S(2)}) collective-permute-start(bf16[3,8,384]{2,1,0:T(8,128)(2,1)S(1)} %get-tuple-element.15), channel_id=1, source_target_pairs={{0,224},{32,64},{64,32},{96,128},{128,96},{160,192},{192,160},{224... | collective-permute-start | bytes 55304 | tf_op jit(solution)/shard_map/ppermute | solution.py:33
  4.9 3.8 %collective-permute-start.1 = (bf16[3,8,384]{2,1,0:T(8,128)(2,1)S(1)}, bf16[3,8,384]{2,1,0:T(8,128)(2,1)S(1)}, u32[]{:S(2)}, u32[]{:S(2)}) collective-permute-start(bf16[3,8,384]{2,1,0:T(8,128)(2,1)S(1)} %get-tuple-element.16), channel_id=1, source_target_pairs={{0,32},{32,0},{64,96},{96,64},{128,160},{160,128},{192,224},{224,1... | collective-permute-start | bytes 55304 | tf_op jit(solution)/shard_map/ppermute | solution.py:34
  8.6 6.0 %copy-start = (bf16[27,384,384]{2,1,0:T(8,128)(2,1)S(1)}, bf16[27,384,384]{2,1,0:T(8,128)(2,1)}, u32[]{:S(2)}) copy-start(bf16[27,384,384]{2,1,0:T(8,128)(2,1)} %param.15) | copy-start | bytes 23887876
  8.6 6.0 %copy-start.1 = (bf16[384,1152]{1,0:T(8,128)(2,1)S(1)}, bf16[384,1152]{1,0:T(8,128)(2,1)}, u32[]{:S(2)}) copy-start(bf16[384,1152]{1,0:T(8,128)(2,1)} %w_qkv.5) | copy-start | bytes 2654212
  8.6 6.0 %copy-start.2 = (bf16[2,8,8,384]{3,2,1,0:T(8,128)(2,1)S(1)}, bf16[2,8,8,384]{3,2,1,0:T(8,128)(2,1)}, u32[]{:S(2)}) copy-start(bf16[2,8,8,384]{3,2,1,0:T(8,128)(2,1)} %cache.1) | copy-start | bytes 294916
  8.6 6.0 %copy-start.4 = (bf16[8,8,384]{2,1,0:T(8,128)(2,1)S(1)}, bf16[8,8,384]{2,1,0:T(8,128)(2,1)}, u32[]{:S(2)}) copy-start(bf16[8,8,384]{2,1,0:T(8,128)(2,1)} %hidden.1) | copy-start | bytes 147460
  8.6 6.0 %copy-start.5 = (bf16[8,8,384]{2,1,0:T(8,128)(2,1)S(1)}, bf16[8,8,384]{2,1,0:T(8,128)(2,1)}, u32[]{:S(2)}) copy-start(bf16[8,8,384]{2,1,0:T(8,128)(2,1)} %param.12) | copy-start | bytes 147460
  8.7 6.0 %copy-start.6 = (f32[1152]{0:T(1024)S(1)}, f32[1152]{0:T(1024)}, u32[]{:S(2)}) copy-start(f32[1152]{0:T(1024)} %b_qkv.5) | copy-start | bytes 13828
  8.7 6.0 %copy-start.7 = (f32[384]{0:T(512)S(1)}, f32[384]{0:T(512)}, u32[]{:S(2)}) copy-start(f32[384]{0:T(512)} %norm_gain.1) | copy-start | bytes 4612
  8.7 6.0 %copy-start.8 = (f32[384]{0:T(512)S(1)}, f32[384]{0:T(512)}, u32[]{:S(2)}) copy-start(f32[384]{0:T(512)} %conv_bias.1) | copy-start | bytes 4612
  8.7 6.0 %copy-start.9 = (f32[384]{0:T(512)S(1)}, f32[384]{0:T(512)}, u32[]{:S(2)}) copy-start(f32[384]{0:T(512)} %attn_gain.1) | copy-start | bytes 4612
  8.8 5.9 %collective-permute-start.2 = (bf16[3,10,384]{2,1,0:T(8,128)(2,1)S(1)}, bf16[3,10,384]{2,1,0:T(8,128)(2,1)S(1)}, u32[]{:S(2)}, u32[]{:S(2)}) collective-permute-start(bf16[3,10,384]{2,1,0:T(8,128)(2,1)S(1)} %get-tuple-element.18), channel_id=1, source_target_pairs={{0,31},{1,2},{2,1},{3,4},{4,3},{5,6},{6,5},{7,8},{8,7},{9,10},{10,... | collective-permute-start | bytes 69128 | tf_op jit(solution)/shard_map/ppermute | solution.py:33
  9.6 5.0 %collective-permute-start.3 = (bf16[3,10,384]{2,1,0:T(8,128)(2,1)S(1)}, bf16[3,10,384]{2,1,0:T(8,128)(2,1)S(1)}, u32[]{:S(2)}, u32[]{:S(2)}) collective-permute-start(bf16[3,10,384]{2,1,0:T(8,128)(2,1)S(1)} %get-tuple-element.19), channel_id=1, source_target_pairs={{0,1},{1,0},{2,3},{3,2},{4,5},{5,4},{6,7},{7,6},{8,9},{9,8},{10,11... | collective-permute-start | bytes 69128 | tf_op jit(solution)/shard_map/ppermute | solution.py:34
  17.3 10.5 %collective-permute-start.4 = (bf16[64,384]{1,0:T(8,128)(2,1)S(1)}, bf16[64,384]{1,0:T(8,128)(2,1)S(1)}, u32[]{:S(2)}, u32[]{:S(2)}) collective-permute-start(bf16[64,384]{1,0:T(8,128)(2,1)S(1)} %get-tuple-element.21.own), channel_id=1, source_target_pairs={{0,16},{4,20},{8,24},{12,28},{16,0},{20,4},{24,8},{28,12},{1,17},{... | collective-permute-start | bytes 147464 | tf_op jit(solution)/shard_map/ppermute | solution.py:341
  23.6 17.8 %all-to-all-start = ((bf16[16,64,384]{2,1,0:T(8,128)(2,1)}), bf16[16,64,384]{2,1,0:T(8,128)(2,1)S(1)}, u32[]{:S(2)}, u32[]{:S(2)}) async-start(bf16[16,64,384]{2,1,0:T(8,128)(2,1)} %bitcast.2), calls=%async_computation | async-start | bytes 1572864 | tf_op jit(solution)/shard_map/all_to_all | solution.py:340
  27.9 34.9 %copy-start.3 = (bf16[384,384]{1,0:T(8,128)(2,1)S(1)}, bf16[384,384]{1,0:T(8,128)(2,1)}, u32[]{:S(2)}) copy-start(bf16[384,384]{1,0:T(8,128)(2,1)} %w_proj.1) | copy-start | bytes 884740
  27.9 34.8 %copy-start.10 = (f32[384]{0:T(512)S(1)}, f32[384]{0:T(512)}, u32[]{:S(2)}) copy-start(f32[384]{0:T(512)} %b_proj.1) | copy-start | bytes 4612
  27.9 5.8 %collective-permute-start.7 = (bf16[128,384]{1,0:T(8,128)(2,1)S(1)}, bf16[128,384]{1,0:T(8,128)(2,1)S(1)}, u32[]{:S(2)}, u32[]{:S(2)}) collective-permute-start(bf16[128,384]{1,0:T(8,128)(2,1)S(1)} %shard_map.112), channel_id=1, source_target_pairs={{0,8},{4,12},{8,0},{12,4},{16,24},{20,28},{24,16},{28,20},{1,9},{5... | collective-permute-start | bytes 294920 | tf_op jit(solution)/shard_map/ppermute | solution.py:342
  29.3 6.9 %collective-permute-start.6 = (bf16[128,384]{1,0:T(8,128)(2,1)S(1)}, bf16[128,384]{1,0:T(8,128)(2,1)S(1)}, u32[]{:S(2)}, u32[]{:S(2)}) collective-permute-start(bf16[128,384]{1,0:T(8,128)(2,1)S(1)} %shard_map.112), channel_id=1, source_target_pairs={{0,28},{4,0},{8,4},{12,8},{16,12},{20,16},{24,20},{28,24},{1,29},{... | collective-permute-start | bytes 294920 | tf_op jit(solution)/shard_map/ppermute | solution.py:342
  30.5 5.8 %collective-permute-start.5 = (bf16[128,384]{1,0:T(8,128)(2,1)S(1)}, bf16[128,384]{1,0:T(8,128)(2,1)S(1)}, u32[]{:S(2)}, u32[]{:S(2)}) collective-permute-start(bf16[128,384]{1,0:T(8,128)(2,1)S(1)} %shard_map.112), channel_id=1, source_target_pairs={{0,4},{4,8},{8,12},{12,16},{16,20},{20,24},{24,28},{28,0},{1,5},{5... | collective-permute-start | bytes 294920 | tf_op jit(solution)/shard_map/ppermute | solution.py:342
  36.3 1.8 %collective-permute-start.8 = (bf16[512,384]{1,0:T(8,128)(2,1)S(1)}, bf16[512,384]{1,0:T(8,128)(2,1)S(1)}, u32[]{:S(2)}, u32[]{:S(2)}) collective-permute-start(bf16[512,384]{1,0:T(8,128)(2,1)S(1)} %pad_maximum_fusion.normed), channel_id=1, source_target_pairs={{0,1},{1,0},{2,3},{3,2},{4,5},{5,4},{6,7},{7,6},{8,9},{9,8},{10,11... | collective-permute-start | bytes 1179656 | tf_op jit(solution)/shard_map/ppermute | solution.py:343

commit v4 on v3

--- a/solution.py
+++ b/solution.py
@@ -124,41 +124,70 @@
     return floats * lax.rsqrt(jnp.mean(floats * floats, axis=-1, keepdims=True) + 1e-06) * gain
 
 
+def conv_input(block, gain):
+    block = rms(block, gain)
+    return (block * jax.nn.sigmoid(block)).astype(BF16).astype(F32)
+
+
+def tap(rows, weight, frame, row, col):
+    start = (9 * frame + 3 * row + col) * C
+    return jnp.dot(
+        rows[row : row + TILE].reshape(PIX, C).astype(BF16),
+        weight[start : start + C],
+        preferred_element_type=F32,
+    )
+
+
+def centre_kernel(cache, hidden, row_outer, row_inner, weight, norm_gain, total, tall):
+    odd = lax.axis_index("ylo")
+    partial = jnp.zeros((PIX, C), F32)
+    for frame in range(3):
+        from_inner = row_inner[frame].astype(F32)
+        from_outer = inside_rows(row_outer[frame].astype(F32))
+        above = jnp.where(odd == 1, from_inner, from_outer)
+        below = jnp.where(odd == 1, from_outer, from_inner)
+        own = (cache[frame] if frame < 2 else hidden[...]).astype(F32)
+        block = jnp.concatenate([above[None], own, below[None]], axis=0)
+        if frame == 2:
+            block = conv_input(block, norm_gain[...].reshape(1, 1, C))
+        tall[frame] = block
+        for row in range(3):
+            partial += tap(block, weight, frame, row, 1)
+    total[...] = partial
+
+
+def centre_stage(cache, hidden, rows, weight, norm_gain):
+    return pl.pallas_call(
+        centre_kernel,
+        out_shape=[
+            jax.ShapeDtypeStruct((PIX, C), F32),
+            jax.ShapeDtypeStruct((3, TILE + 2, TILE, C), F32),
+        ],
+        compiler_params=pltpu.CompilerParams(vmem_limit_bytes=16 << 20),
+        cost_estimate=pl.CostEstimate(flops=1 << 31, bytes_accessed=1 << 20, transcendentals=0),
+    )(cache, hidden, *rows[::-1], weight, norm_gain)
+
+
 def conv_kernel(
-    cache, hidden, row_outer, row_inner, col_outer, col_inner, weight, skip,
-    norm_gain, conv_bias, attn_gain, w_qkv, b_qkv, middle, normed, queries, wide, shifted,
+    centre, tall, col_outer, col_inner, weight, skip,
+    norm_gain, conv_bias, attn_gain, w_qkv, b_qkv, middle, normed, queries, wide,
 ):
-    row_odd = lax.axis_index("ylo")
     odd = lax.axis_index("core")
-    total = jnp.zeros((PIX, C), F32)
+    total = centre[...]
     for frame in range(3):
-        own = cache[frame] if frame < 2 else hidden[...]
-        wide[pl.ds(1, TILE), 1 : 1 + TILE] = own.astype(F32)
-        wide[9 - 9 * row_odd, 1 : 1 + TILE] = row_inner[frame].astype(F32)
-        wide[9 * row_odd, 1 : 1 + TILE] = inside_rows(row_outer[frame].astype(F32))
         from_inner = col_inner[frame].astype(F32)
         from_outer = inside_cols(col_outer[frame].astype(F32))
-        wide[:, 0] = jnp.where(odd == 1, from_inner, from_outer)
-        wide[:, 1 + TILE] = jnp.where(odd == 1, from_outer, from_inner)
-        block = wide[:, 0 : TILE + 2]
+        left = jnp.where(odd == 1, from_inner, from_outer)
+        right = jnp.where(odd == 1, from_outer, from_inner)
         if frame == 2:
-            block = rms(block, norm_gain[...].reshape(1, 1, C))
-            block = (block * jax.nn.sigmoid(block)).astype(BF16).astype(F32)
-        for col in range(3):
-            shifted[frame, col] = block[:, col : col + TILE, :]
-    for frame in range(3):
-        for row in range(3):
-            tap = 9 * frame + 3 * row
-            window = jnp.concatenate(
-                [
-                    shifted[frame, col, row : row + TILE].reshape(PIX, C).astype(BF16)
-                    for col in range(3)
-                ],
-                axis=1,
-            )
-            total += jnp.dot(
-                window, weight[tap * C : (tap + 3) * C], preferred_element_type=F32
-            )
+            left, right = conv_input(left, norm_gain[...]), conv_input(right, norm_gain[...])
+        wide[:, 1 : 1 + TILE] = tall[frame]
+        wide[:, 0] = left
+        wide[:, 1 + TILE] = right
+        for col in (0, 2):
+            block = wide[:, col : col + TILE]
+            for row in range(3):
+                total += tap(block, weight, frame, row, col)
     mid = (skip[...].astype(F32) + (total + conv_bias[...])).astype(BF16)
     middle[...] = mid
     norm = rms(mid.astype(F32), attn_gain[...]).astype(BF16)
@@ -168,17 +197,14 @@
         queries[place * PIX : (place + 1) * PIX] = query
 
 
-def conv_stage(cache, hidden, rows, cols, weight, skip, norm_gain, conv_bias, attn_gain, w_qkv, b_qkv):
+def conv_stage(centre, cols, weight, skip, norm_gain, conv_bias, attn_gain, w_qkv, b_qkv):
     out = jax.ShapeDtypeStruct((PIX, C), BF16)
     return pl.pallas_call(
         conv_kernel,
         out_shape=[out, out, jax.ShapeDtypeStruct((QUERIES, C), BF16)],
-        scratch_shapes=[
-            pltpu.VMEM((TILE + 2, 2 * TILE, C), F32),
-            pltpu.VMEM((3, 3, TILE + 2, TILE, C), F32),
-        ],
+        scratch_shapes=[pltpu.VMEM((TILE + 2, 2 * TILE, C), F32)],
         compiler_params=pltpu.CompilerParams(vmem_limit_bytes=24 << 20),
-    )(cache, hidden, *rows[::-1], *cols[::-1], weight, skip, norm_gain, conv_bias, attn_gain, w_qkv, b_qkv)
+    )(*centre, *cols[::-1], weight, skip, norm_gain, conv_bias, attn_gain, w_qkv, b_qkv)
 
 
 def pair_kernel(own, far, both):
@@ -324,12 +350,11 @@
     edges, own_sides = own_edges(cache_frames, hidden_in)
     rows = swapped(edges, ROW)
     cols = swapped(column_edges(own_sides, *rows), COL)
+    weight = conv_weight.reshape(27 * C, C)
     middle, normed, queries = conv_stage(
-        cache_frames,
-        hidden_in,
-        rows,
+        centre_stage(cache_frames, hidden_in, rows, weight, norm_gain),
         cols,
-        conv_weight.reshape(27 * C, C),
+        weight,
         skip_input.reshape(PIX, C),
         norm_gain,
         conv_bias,

time: 64.2 us -> 63.8 us (level)
  transfers between devices with their start and end apart: 10 -> 10, of which waited for: 7 -> 7; matrix products, arithmetic and copies ran while one was open for 0% -> 0% of each run, Pallas kernels for 1% -> 2%
where the time goes in v4:
time: 63.8 us; the launch traced here: 63.6 us
  starting transfers between devices  21 us (33%)
  blocking collectives  18.1 us (28%)
  waiting for transfers between devices  15.3 us (24%)
  Pallas kernels  8.91 us (14%)
    all_to_all x1, blocking collectives, shards(): partials = lax.all_to_all(partial, PLANE, 0, 0, tiled=True)  18.1 us
    ppermute x1, starting transfers between devices, shards(): far = pair_stage(normed, lax.ppermute(normed, 'z', flips(4)))  6.29 us
    ppermute x3, waiting for transfers between devices, shards(): lax.ppermute(far, 'z', links)  4.9 us
    ppermute x2, starting transfers between devices, swapped(): far = lax.ppermute(edges[1], axes, outer)  4.74 us
    ppermute x2, waiting for transfers between devices, swapped(): far = lax.ppermute(edges[1], axes, outer)  4.26 us
    all_to_all x1, starting transfers between devices, shards(): all_queries = lax.all_to_all(queries, PLANE, 0, 0, tiled=True)  4.2 us
    ppermute x3, starting transfers between devices, shards(): lax.ppermute(far, 'z', links)  3.43 us
    all_to_all x1, waiting for transfers between devices, shards(): all_queries = lax.all_to_all(queries, PLANE, 0, 0, tiled=True)  3.39 us
  transfers between devices with their start and end apart: 10, of which 7 were waited for; matrix products, arithmetic and copies ran while one was open for 0% of the time, Pallas kernels for 2%

profile of v4, /device:TPU:32, one launch (start us, length us, event | category | flops | bytes accessed | tf_op | source)
XLA Modules:
  0.0 63.6 jit_solution(1441701721626535172)
XLA Ops:
  0.0 1.0 %shard_map.109 = (bf16[3,8,384]{2,1,0:T(8,128)(2,1)S(1)}, bf16[3,8,384]{2,1,0:T(8,128)(2,1)S(1)}, bf16[2,3,8,384]{3,2,1,0:T(8,128)(2,1)S(1)}) custom-call(bf16[2,8,8,384]{3,2,1,0:T(8,128)(2,1)} %cache.1, bf16[8,8,384]{2,1,0:T(8,128)(2,1)} %hidden.1), custom_call_target="tpu_custom_call" | custom-call | tf_op jit(solution)/shard_map/pallas_call | solution.py:80
  1.0 3.9 %collective-permute-start = (bf16[3,8,384]{2,1,0:T(8,128)(2,1)S(1)}, bf16[3,8,384]{2,1,0:T(8,128)(2,1)S(1)}, u32[]{:S(2)}, u32[]{:S(2)}) collective-permute-start(bf16[3,8,384]{2,1,0:T(8,128)(2,1)S(1)} %get-tuple-element.17), channel_id=1, source_target_pairs={{0,224},{32,64},{64,32},{96,128},{128,96},{160,192},{192,160},{224... | collective-permute-start | bytes 55304 | tf_op jit(solution)/shard_map/ppermute | solution.py:33
  4.9 2.1 %collective-permute-done.row_outer = bf16[3,8,384]{2,1,0:T(8,128)(2,1)S(1)} collective-permute-done((bf16[3,8,384]{2,1,0:T(8,128)(2,1)S(1)}, bf16[3,8,384]{2,1,0:T(8,128)(2,1)S(1)}, u32[]{:S(2)}, u32[]{:S(2)}) %collective-permute-start) | collective-permute-done | bytes 18464 | tf_op jit(solution)/shard_map/ppermute | solution.py:33
  7.0 1.7 %collective-permute-done.1.row_inner = bf16[3,8,384]{2,1,0:T(8,128)(2,1)S(1)} collective-permute-done((bf16[3,8,384]{2,1,0:T(8,128)(2,1)S(1)}, bf16[3,8,384]{2,1,0:T(8,128)(2,1)S(1)}, u32[]{:S(2)}, u32[]{:S(2)}) %collective-permute-start.1) | collective-permute-done | bytes 18464 | tf_op jit(solution)/shard_map/ppermute | solution.py:34
  8.7 0.0 copy-start.1
  8.7 0.0 copy-start.5
  8.7 0.0 copy-start.6
  8.7 0.0 copy-start.9
  8.7 0.0 copy-start.10
  8.8 0.9 %collective-permute-start.2 = (bf16[3,10,384]{2,1,0:T(8,128)(2,1)S(1)}, bf16[3,10,384]{2,1,0:T(8,128)(2,1)S(1)}, u32[]{:S(2)}, u32[]{:S(2)}) collective-permute-start(bf16[3,10,384]{2,1,0:T(8,128)(2,1)S(1)} %get-tuple-element.22), channel_id=1, source_target_pairs={{0,31},{1,2},{2,1},{3,4},{4,3},{5,6},{6,5},{7,8},{8,7},{9,10},{10,... | collective-permute-start | bytes 69128 | tf_op jit(solution)/shard_map/ppermute | solution.py:33
  9.6 2.2 %collective-permute-start.3 = (bf16[3,10,384]{2,1,0:T(8,128)(2,1)S(1)}, bf16[3,10,384]{2,1,0:T(8,128)(2,1)S(1)}, u32[]{:S(2)}, u32[]{:S(2)}) collective-permute-start(bf16[3,10,384]{2,1,0:T(8,128)(2,1)S(1)} %get-tuple-element.23), channel_id=1, source_target_pairs={{0,1},{1,0},{2,3},{3,2},{4,5},{5,4},{6,7},{7,6},{8,9},{9,8},{10,11... | collective-permute-start | bytes 69128 | tf_op jit(solution)/shard_map/ppermute | solution.py:34
  11.9 0.0 copy-done
  11.9 0.5 shard_map.110
  12.5 2.2 %collective-permute-done.2.col_outer = bf16[3,10,384]{2,1,0:T(8,128)(2,1)S(1)} collective-permute-done((bf16[3,10,384]{2,1,0:T(8,128)(2,1)S(1)}, bf16[3,10,384]{2,1,0:T(8,128)(2,1)S(1)}, u32[]{:S(2)}, u32[]{:S(2)}) %collective-permute-start.2) | collective-permute-done | bytes 23072 | tf_op jit(solution)/shard_map/ppermute | solution.py:33
  14.7 2.3 %shard_map.112 = (bf16[64,384]{1,0:T(8,128)(2,1)S(1)}, bf16[64,384]{1,0:T(8,128)(2,1)S(1)}, bf16[1024,384]{1,0:T(8,128)(2,1)}) custom-call(f32[64,384]{1,0:T(8,128)S(1)} %get-tuple-element.19.centre, f32[3,10,8,384]{3,2,1,0:T(8,128)S(1)} %get-tuple-element.20.tall, bf16[3,10,384]{2,1,0:T(8,128)(2,1)S(1)} %collective-permute-done.2.col_outer, ...), custom_call_target="tpu_custom_call" | custom-call | tf_op jit(solution)/shard_map/pallas_call | solution.py:202
  17.0 6.3 %collective-permute-start.4 = (bf16[64,384]{1,0:T(8,128)(2,1)S(1)}, bf16[64,384]{1,0:T(8,128)(2,1)S(1)}, u32[]{:S(2)}, u32[]{:S(2)}) collective-permute-start(bf16[64,384]{1,0:T(8,128)(2,1)S(1)} %get-tuple-element.25.own), channel_id=1, source_target_pairs={{0,16},{4,20},{8,24},{12,28},{16,0},{20,4},{24,8},{28,12},{1,17},{... | collective-permute-start | bytes 147464 | tf_op jit(solution)/shard_map/ppermute | solution.py:366
  23.3 4.2 %all-to-all-start = ((bf16[16,64,384]{2,1,0:T(8,128)(2,1)}), bf16[16,64,384]{2,1,0:T(8,128)(2,1)S(1)}, u32[]{:S(2)}, u32[]{:S(2)}) async-start(bf16[16,64,384]{2,1,0:T(8,128)(2,1)} %bitcast.2), calls=%async_computation | async-start | bytes 1572864 | tf_op jit(solution)/shard_map/all_to_all | solution.py:365
  27.5 0.0 collective-permute-done.4.far
  27.5 0.0 copy-start.3
  27.5 0.0 copy-start.8
  27.5 1.4 %collective-permute-start.7 = (bf16[128,384]{1,0:T(8,128)(2,1)S(1)}, bf16[128,384]{1,0:T(8,128)(2,1)S(1)}, u32[]{:S(2)}, u32[]{:S(2)}) collective-permute-start(bf16[128,384]{1,0:T(8,128)(2,1)S(1)} %shard_map.113), channel_id=1, source_target_pairs={{0,8},{4,12},{8,0},{12,4},{16,24},{20,28},{24,16},{28,20},{1,9},{5... | collective-permute-start | bytes 294920 | tf_op jit(solution)/shard_map/ppermute | solution.py:367
  28.9 1.2 %collective-permute-start.6 = (bf16[128,384]{1,0:T(8,128)(2,1)S(1)}, bf16[128,384]{1,0:T(8,128)(2,1)S(1)}, u32[]{:S(2)}, u32[]{:S(2)}) collective-permute-start(bf16[128,384]{1,0:T(8,128)(2,1)S(1)} %shard_map.113), channel_id=1, source_target_pairs={{0,28},{4,0},{8,4},{12,8},{16,12},{20,16},{24,20},{28,24},{1,29},{... | collective-permute-start | bytes 294920 | tf_op jit(solution)/shard_map/ppermute | solution.py:367
  30.1 0.9 %collective-permute-start.5 = (bf16[128,384]{1,0:T(8,128)(2,1)S(1)}, bf16[128,384]{1,0:T(8,128)(2,1)S(1)}, u32[]{:S(2)}, u32[]{:S(2)}) collective-permute-start(bf16[128,384]{1,0:T(8,128)(2,1)S(1)} %shard_map.113), channel_id=1, source_target_pairs={{0,4},{4,8},{8,12},{12,16},{16,20},{20,24},{24,28},{28,0},{1,5},{5... | collective-permute-start | bytes 294920 | tf_op jit(solution)/shard_map/ppermute | solution.py:367
  31.0 2.4 %collective-permute-done.7 = bf16[128,384]{1,0:T(8,128)(2,1)S(1)} collective-permute-done((bf16[128,384]{1,0:T(8,128)(2,1)S(1)}, bf16[128,384]{1,0:T(8,128)(2,1)S(1)}, u32[]{:S(2)}, u32[]{:S(2)}) %collective-permute-start.7) | collective-permute-done | bytes 98336 | tf_op jit(solution)/shard_map/ppermute | solution.py:367
  33.3 2.5 %collective-permute-done.6 = bf16[128,384]{1,0:T(8,128)(2,1)S(1)} collective-permute-done((bf16[128,384]{1,0:T(8,128)(2,1)S(1)}, bf16[128,384]{1,0:T(8,128)(2,1)S(1)}, u32[]{:S(2)}, u32[]{:S(2)}) %collective-permute-start.6) | collective-permute-done | bytes 98336 | tf_op jit(solution)/shard_map/ppermute | solution.py:367
  35.9 0.1 collective-permute-start.8
  36.0 0.6 %shard_map.114 = (bf16[512,384]{1,0:T(8,128)(2,1)S(1)}, bf16[384,512]{1,0:T(8,128)(2,1)S(1)}) custom-call(bf16[512,384]{1,0:T(8,128)(2,1)S(1)} %pad_maximum_fusion.normed, bf16[384,1152]{1,0:T(8,128)(2,1)S(1)} %copy-done.1, f32[1152]{0:T(1024)S(1)} %copy-done.6), custom_call_target="tpu_custom_call" | custom-call | flops 1073741824 | bytes 1048576 | tf_op jit(solution)/shard_map/pallas_call | solution.py:244
  36.7 1.1 %collective-permute-done.8.other = bf16[512,384]{1,0:T(8,128)(2,1)S(1)} collective-permute-done((bf16[512,384]{1,0:T(8,128)(2,1)S(1)}, bf16[512,384]{1,0:T(8,128)(2,1)S(1)}, u32[]{:S(2)}, u32[]{:S(2)}) %collective-permute-start.8) | collective-permute-done | bytes 393248 | tf_op jit(solution)/shard_map/ppermute | solution.py:368
  37.7 3.4 %all-to-all-done = bf16[16,64,384]{2,1,0:T(8,128)(2,1)S(1)} async-done(((bf16[16,64,384]{2,1,0:T(8,128)(2,1)}), bf16[16,64,384]{2,1,0:T(8,128)(2,1)S(1)}, u32[]{:S(2)}, u32[]{:S(2)}) %all-to-all-start) | async-done | bytes 786464 | tf_op jit(solution)/shard_map/all_to_all | solution.py:365
  41.1 3.2 %shard_map.115 = bf16[16,200,128]{2,1,0:T(8,128)(2,1)S(1)} custom-call(bf16[1024,384]{1,0:T(8,128)(2,1)S(1)} %bitcast.7, bf16[512,384]{1,0:T(8,128)(2,1)S(1)} %get-tuple-element.26.line_keys, bf16[384,512]{1,0:T(8,128)(2,1)S(1)} %get-tuple-element.27.line_values, bf16[512,384]{1,0:T(8,128)(2,1)S(1)} %collective-permute-done.8.other, ...), custom_call_target="tpu_custom_call" | custom-call | tf_op jit(solution)/shard_map/pallas_call | solution.py:290
  44.3 18.1 %all_to_all.16.partials = bf16[16,200,128]{2,1,0:T(8,128)(2,1)S(1)} all-to-all(bf16[16,200,128]{2,1,0:T(8,128)(2,1)S(1)} %shard_map.115), channel_id=1, replica_groups=mesh['x'=4,'ylo'=2,'z'=8,'yhi'=2,'core'=2] {'x','yhi','ylo'}, dimensions={0} | all-to-all | bytes 1638400 | tf_op jit(solution)/shard_map/all_to_all | solution.py:376
  62.4 1.2 %shard_map.116 = bf16[64,384]{1,0:T(8,128)(2,1)} custom-call(bf16[16,200,128]{2,1,0:T(8,128)(2,1)S(1)} %all_to_all.16.partials, bf16[64,384]{1,0:T(8,128)(2,1)S(1)} %get-tuple-element.28.middle, bf16[384,384]{1,0:T(8,128)(2,1)S(1)} %copy-done.3, f32[384]{0:T(512)S(1)} %copy-done.8), custom_call_target="tpu_custom_call" | custom-call | tf_op jit(solution)/shard_map/pallas_call | solution.py:322
  (20 shorter events, 0.1 us)
Async XLA Ops:
  1.0 6.0 %collective-permute-start = (bf16[3,8,384]{2,1,0:T(8,128)(2,1)S(1)}, bf16[3,8,384]{2,1,0:T(8,128)(2,1)S(1)}, u32[]{:S(2)}, u32[]{:S(2)}) collective-permute-start(bf16[3,8,384]{2,1,0:T(8,128)(2,1)S(1)} %get-tuple-element.17), channel_id=1, source_target_pairs={{0,224},{32,64},{64,32},{96,128},{128,96},{160,192},{192,160},{224... | collective-permute-start | bytes 55304 | tf_op jit(solution)/shard_map/ppermute | solution.py:33
  4.9 3.8 %collective-permute-start.1 = (bf16[3,8,384]{2,1,0:T(8,128)(2,1)S(1)}, bf16[3,8,384]{2,1,0:T(8,128)(2,1)S(1)}, u32[]{:S(2)}, u32[]{:S(2)}) collective-permute-start(bf16[3,8,384]{2,1,0:T(8,128)(2,1)S(1)} %get-tuple-element.18), channel_id=1, source_target_pairs={{0,32},{32,0},{64,96},{96,64},{128,160},{160,128},{192,224},{224,1... | collective-permute-start | bytes 55304 | tf_op jit(solution)/shard_map/ppermute | solution.py:34
  8.6 3.3 %copy-start = (bf16[27,384,384]{2,1,0:T(8,128)(2,1)S(1)}, bf16[27,384,384]{2,1,0:T(8,128)(2,1)}, u32[]{:S(2)}) copy-start(bf16[27,384,384]{2,1,0:T(8,128)(2,1)} %param.15) | copy-start | bytes 23887876
  8.6 3.3 %copy-start.2 = (bf16[2,8,8,384]{3,2,1,0:T(8,128)(2,1)S(1)}, bf16[2,8,8,384]{3,2,1,0:T(8,128)(2,1)}, u32[]{:S(2)}) copy-start(bf16[2,8,8,384]{3,2,1,0:T(8,128)(2,1)} %cache.1) | copy-start | bytes 294916
  8.6 3.3 %copy-start.4 = (bf16[8,8,384]{2,1,0:T(8,128)(2,1)S(1)}, bf16[8,8,384]{2,1,0:T(8,128)(2,1)}, u32[]{:S(2)}) copy-start(bf16[8,8,384]{2,1,0:T(8,128)(2,1)} %hidden.1) | copy-start | bytes 147460
  8.6 3.3 %copy-start.7 = (f32[384]{0:T(512)S(1)}, f32[384]{0:T(512)}, u32[]{:S(2)}) copy-start(f32[384]{0:T(512)} %norm_gain.3) | copy-start | bytes 4612
  8.7 5.9 %copy-start.1 = (bf16[384,1152]{1,0:T(8,128)(2,1)S(1)}, bf16[384,1152]{1,0:T(8,128)(2,1)}, u32[]{:S(2)}) copy-start(bf16[384,1152]{1,0:T(8,128)(2,1)} %w_qkv.5) | copy-start | bytes 2654212
  8.7 5.9 %copy-start.5 = (bf16[8,8,384]{2,1,0:T(8,128)(2,1)S(1)}, bf16[8,8,384]{2,1,0:T(8,128)(2,1)}, u32[]{:S(2)}) copy-start(bf16[8,8,384]{2,1,0:T(8,128)(2,1)} %param.12) | copy-start | bytes 147460
  8.7 5.9 %copy-start.6 = (f32[1152]{0:T(1024)S(1)}, f32[1152]{0:T(1024)}, u32[]{:S(2)}) copy-start(f32[1152]{0:T(1024)} %b_qkv.5) | copy-start | bytes 13828
  8.7 5.9 %copy-start.9 = (f32[384]{0:T(512)S(1)}, f32[384]{0:T(512)}, u32[]{:S(2)}) copy-start(f32[384]{0:T(512)} %conv_bias.1) | copy-start | bytes 4612
  8.7 5.9 %copy-start.10 = (f32[384]{0:T(512)S(1)}, f32[384]{0:T(512)}, u32[]{:S(2)}) copy-start(f32[384]{0:T(512)} %attn_gain.1) | copy-start | bytes 4612
  8.8 5.9 %collective-permute-start.2 = (bf16[3,10,384]{2,1,0:T(8,128)(2,1)S(1)}, bf16[3,10,384]{2,1,0:T(8,128)(2,1)S(1)}, u32[]{:S(2)}, u32[]{:S(2)}) collective-permute-start(bf16[3,10,384]{2,1,0:T(8,128)(2,1)S(1)} %get-tuple-element.22), channel_id=1, source_target_pairs={{0,31},{1,2},{2,1},{3,4},{4,3},{5,6},{6,5},{7,8},{8,7},{9,10},{10,... | collective-permute-start | bytes 69128 | tf_op jit(solution)/shard_map/ppermute | solution.py:33
  9.6 5.0 %collective-permute-start.3 = (bf16[3,10,384]{2,1,0:T(8,128)(2,1)S(1)}, bf16[3,10,384]{2,1,0:T(8,128)(2,1)S(1)}, u32[]{:S(2)}, u32[]{:S(2)}) collective-permute-start(bf16[3,10,384]{2,1,0:T(8,128)(2,1)S(1)} %get-tuple-element.23), channel_id=1, source_target_pairs={{0,1},{1,0},{2,3},{3,2},{4,5},{5,4},{6,7},{7,6},{8,9},{9,8},{10,11... | collective-permute-start | bytes 69128 | tf_op jit(solution)/shard_map/ppermute | solution.py:34
  17.0 10.5 %collective-permute-start.4 = (bf16[64,384]{1,0:T(8,128)(2,1)S(1)}, bf16[64,384]{1,0:T(8,128)(2,1)S(1)}, u32[]{:S(2)}, u32[]{:S(2)}) collective-permute-start(bf16[64,384]{1,0:T(8,128)(2,1)S(1)} %get-tuple-element.25.own), channel_id=1, source_target_pairs={{0,16},{4,20},{8,24},{12,28},{16,0},{20,4},{24,8},{28,12},{1,17},{... | collective-permute-start | bytes 147464 | tf_op jit(solution)/shard_map/ppermute | solution.py:366
  23.3 17.8 %all-to-all-start = ((bf16[16,64,384]{2,1,0:T(8,128)(2,1)}), bf16[16,64,384]{2,1,0:T(8,128)(2,1)S(1)}, u32[]{:S(2)}, u32[]{:S(2)}) async-start(bf16[16,64,384]{2,1,0:T(8,128)(2,1)} %bitcast.2), calls=%async_computation | async-start | bytes 1572864 | tf_op jit(solution)/shard_map/all_to_all | solution.py:365
  27.5 34.9 %copy-start.3 = (bf16[384,384]{1,0:T(8,128)(2,1)S(1)}, bf16[384,384]{1,0:T(8,128)(2,1)}, u32[]{:S(2)}) copy-start(bf16[384,384]{1,0:T(8,128)(2,1)} %w_proj.1) | copy-start | bytes 884740
  27.5 34.8 %copy-start.8 = (f32[384]{0:T(512)S(1)}, f32[384]{0:T(512)}, u32[]{:S(2)}) copy-start(f32[384]{0:T(512)} %b_proj.1) | copy-start | bytes 4612
  27.5 5.8 %collective-permute-start.7 = (bf16[128,384]{1,0:T(8,128)(2,1)S(1)}, bf16[128,384]{1,0:T(8,128)(2,1)S(1)}, u32[]{:S(2)}, u32[]{:S(2)}) collective-permute-start(bf16[128,384]{1,0:T(8,128)(2,1)S(1)} %shard_map.113), channel_id=1, source_target_pairs={{0,8},{4,12},{8,0},{12,4},{16,24},{20,28},{24,16},{28,20},{1,9},{5... | collective-permute-start | bytes 294920 | tf_op jit(solution)/shard_map/ppermute | solution.py:367
  28.9 6.9 %collective-permute-start.6 = (bf16[128,384]{1,0:T(8,128)(2,1)S(1)}, bf16[128,384]{1,0:T(8,128)(2,1)S(1)}, u32[]{:S(2)}, u32[]{:S(2)}) collective-permute-start(bf16[128,384]{1,0:T(8,128)(2,1)S(1)} %shard_map.113), channel_id=1, source_target_pairs={{0,28},{4,0},{8,4},{12,8},{16,12},{20,16},{24,20},{28,24},{1,29},{... | collective-permute-start | bytes 294920 | tf_op jit(solution)/shard_map/ppermute | solution.py:367
  30.1 5.8 %collective-permute-start.5 = (bf16[128,384]{1,0:T(8,128)(2,1)S(1)}, bf16[128,384]{1,0:T(8,128)(2,1)S(1)}, u32[]{:S(2)}, u32[]{:S(2)}) collective-permute-start(bf16[128,384]{1,0:T(8,128)(2,1)S(1)} %shard_map.113), channel_id=1, source_target_pairs={{0,4},{4,8},{8,12},{12,16},{16,20},{20,24},{24,28},{28,0},{1,5},{5... | collective-permute-start | bytes 294920 | tf_op jit(solution)/shard_map/ppermute | solution.py:367
  35.9 1.8 %collective-permute-start.8 = (bf16[512,384]{1,0:T(8,128)(2,1)S(1)}, bf16[512,384]{1,0:T(8,128)(2,1)S(1)}, u32[]{:S(2)}, u32[]{:S(2)}) collective-permute-start(bf16[512,384]{1,0:T(8,128)(2,1)S(1)} %pad_maximum_fusion.normed), channel_id=1, source_target_pairs={{0,1},{1,0},{2,3},{3,2},{4,5},{5,4},{6,7},{7,6},{8,9},{9,8},{10,11... | collective-permute-start | bytes 1179656 | tf_op jit(solution)/shard_map/ppermute | solution.py:368

commit v5 on v4

--- a/solution.py
+++ b/solution.py
@@ -174,6 +174,7 @@
 ):
     odd = lax.axis_index("core")
     total = centre[...]
+    windows = []
     for frame in range(3):
         from_inner = col_inner[frame].astype(F32)
         from_outer = inside_cols(col_outer[frame].astype(F32))
@@ -184,10 +185,18 @@
         wide[:, 1 : 1 + TILE] = tall[frame]
         wide[:, 0] = left
         wide[:, 1 + TILE] = right
-        for col in (0, 2):
-            block = wide[:, col : col + TILE]
-            for row in range(3):
-                total += tap(block, weight, frame, row, col)
+        blocks = [wide[:, col : col + TILE] for col in (0, 2)]
+        for row in range(3):
+            for col, block in zip((0, 2), blocks):
+                window = block[row : row + TILE].reshape(PIX, C).astype(BF16)
+                windows.append((9 * frame + 3 * row + col, window))
+    for group in [windows[:1]] + [windows[i : i + 2] for i in range(1, len(windows), 2)]:
+        start = group[0][0] * C
+        total += jnp.dot(
+            jnp.concatenate([window for _, window in group], axis=1),
+            weight[start : start + len(group) * C],
+            preferred_element_type=F32,
+        )
     mid = (skip[...].astype(F32) + (total + conv_bias[...])).astype(BF16)
     middle[...] = mid
     norm = rms(mid.astype(F32), attn_gain[...]).astype(BF16)

time: 63.8 us -> 63.7 us (level)
  no operation moved by 1% of the time
where the time goes in v5:
time: 63.7 us; the launch traced here: 63.5 us
  starting transfers between devices  21 us (33%)
  blocking collectives  18.1 us (28%)
  waiting for transfers between devices  15.3 us (24%)
  Pallas kernels  8.84 us (14%)
    all_to_all x1, blocking collectives, shards(): partials = lax.all_to_all(partial, PLANE, 0, 0, tiled=True)  18.1 us
    ppermute x1, starting transfers between devices, shards(): far = pair_stage(normed, lax.ppermute(normed, 'z', flips(4)))  6.29 us
    ppermute x3, waiting for transfers between devices, shards(): lax.ppermute(far, 'z', links)  4.9 us
    ppermute x2, starting transfers between devices, swapped(): far = lax.ppermute(edges[1], axes, outer)  4.74 us
    ppermute x2, waiting for transfers between devices, swapped(): far = lax.ppermute(edges[1], axes, outer)  4.26 us
    all_to_all x1, starting transfers between devices, shards(): all_queries = lax.all_to_all(queries, PLANE, 0, 0, tiled=True)  4.21 us
    ppermute x3, starting transfers between devices, shards(): lax.ppermute(far, 'z', links)  3.43 us
    all_to_all x1, waiting for transfers between devices, shards(): all_queries = lax.all_to_all(queries, PLANE, 0, 0, tiled=True)  3.38 us
  transfers between devices with their start and end apart: 10, of which 7 were waited for; matrix products, arithmetic and copies ran while one was open for 0% of the time, Pallas kernels for 2%

profile of v5, /device:TPU:32, one launch (start us, length us, event | category | flops | bytes accessed | tf_op | source)
XLA Modules:
  0.0 63.5 jit_solution(4849238577951364027)
XLA Ops:
  0.0 1.0 %shard_map.109 = (bf16[3,8,384]{2,1,0:T(8,128)(2,1)S(1)}, bf16[3,8,384]{2,1,0:T(8,128)(2,1)S(1)}, bf16[2,3,8,384]{3,2,1,0:T(8,128)(2,1)S(1)}) custom-call(bf16[2,8,8,384]{3,2,1,0:T(8,128)(2,1)} %cache.1, bf16[8,8,384]{2,1,0:T(8,128)(2,1)} %hidden.1), custom_call_target="tpu_custom_call" | custom-call | tf_op jit(solution)/shard_map/pallas_call | solution.py:80
  1.0 3.9 %collective-permute-start = (bf16[3,8,384]{2,1,0:T(8,128)(2,1)S(1)}, bf16[3,8,384]{2,1,0:T(8,128)(2,1)S(1)}, u32[]{:S(2)}, u32[]{:S(2)}) collective-permute-start(bf16[3,8,384]{2,1,0:T(8,128)(2,1)S(1)} %get-tuple-element.17), channel_id=1, source_target_pairs={{0,224},{32,64},{64,32},{96,128},{128,96},{160,192},{192,160},{224... | collective-permute-start | bytes 55304 | tf_op jit(solution)/shard_map/ppermute | solution.py:33
  4.9 0.0 collective-permute-start.1
  4.9 2.1 %collective-permute-done.row_outer = bf16[3,8,384]{2,1,0:T(8,128)(2,1)S(1)} collective-permute-done((bf16[3,8,384]{2,1,0:T(8,128)(2,1)S(1)}, bf16[3,8,384]{2,1,0:T(8,128)(2,1)S(1)}, u32[]{:S(2)}, u32[]{:S(2)}) %collective-permute-start) | collective-permute-done | bytes 18464 | tf_op jit(solution)/shard_map/ppermute | solution.py:33
  7.0 1.7 %collective-permute-done.1.row_inner = bf16[3,8,384]{2,1,0:T(8,128)(2,1)S(1)} collective-permute-done((bf16[3,8,384]{2,1,0:T(8,128)(2,1)S(1)}, bf16[3,8,384]{2,1,0:T(8,128)(2,1)S(1)}, u32[]{:S(2)}, u32[]{:S(2)}) %collective-permute-start.1) | collective-permute-done | bytes 18464 | tf_op jit(solution)/shard_map/ppermute | solution.py:34
  8.7 0.0 copy-start.1
  8.7 0.0 copy-start.5
  8.7 0.0 copy-start.6
  8.7 0.0 copy-start.9
  8.7 0.0 copy-start.10
  8.8 0.9 %collective-permute-start.2 = (bf16[3,10,384]{2,1,0:T(8,128)(2,1)S(1)}, bf16[3,10,384]{2,1,0:T(8,128)(2,1)S(1)}, u32[]{:S(2)}, u32[]{:S(2)}) collective-permute-start(bf16[3,10,384]{2,1,0:T(8,128)(2,1)S(1)} %get-tuple-element.22), channel_id=1, source_target_pairs={{0,31},{1,2},{2,1},{3,4},{4,3},{5,6},{6,5},{7,8},{8,7},{9,10},{10,... | collective-permute-start | bytes 69128 | tf_op jit(solution)/shard_map/ppermute | solution.py:33
  9.6 2.2 %collective-permute-start.3 = (bf16[3,10,384]{2,1,0:T(8,128)(2,1)S(1)}, bf16[3,10,384]{2,1,0:T(8,128)(2,1)S(1)}, u32[]{:S(2)}, u32[]{:S(2)}) collective-permute-start(bf16[3,10,384]{2,1,0:T(8,128)(2,1)S(1)} %get-tuple-element.23), channel_id=1, source_target_pairs={{0,1},{1,0},{2,3},{3,2},{4,5},{5,4},{6,7},{7,6},{8,9},{9,8},{10,11... | collective-permute-start | bytes 69128 | tf_op jit(solution)/shard_map/ppermute | solution.py:34
  11.9 0.0 copy-done
  11.9 0.5 shard_map.110
  12.5 2.2 %collective-permute-done.2.col_outer = bf16[3,10,384]{2,1,0:T(8,128)(2,1)S(1)} collective-permute-done((bf16[3,10,384]{2,1,0:T(8,128)(2,1)S(1)}, bf16[3,10,384]{2,1,0:T(8,128)(2,1)S(1)}, u32[]{:S(2)}, u32[]{:S(2)}) %collective-permute-start.2) | collective-permute-done | bytes 23072 | tf_op jit(solution)/shard_map/ppermute | solution.py:33
  14.7 2.2 %shard_map.112 = (bf16[64,384]{1,0:T(8,128)(2,1)S(1)}, bf16[64,384]{1,0:T(8,128)(2,1)S(1)}, bf16[1024,384]{1,0:T(8,128)(2,1)}) custom-call(f32[64,384]{1,0:T(8,128)S(1)} %get-tuple-element.19.centre, f32[3,10,8,384]{3,2,1,0:T(8,128)S(1)} %get-tuple-element.20.tall, bf16[3,10,384]{2,1,0:T(8,128)(2,1)S(1)} %collective-permute-done.2.col_outer, ...), custom_call_target="tpu_custom_call" | custom-call | tf_op jit(solution)/shard_map/pallas_call | solution.py:211
  16.9 6.3 %collective-permute-start.4 = (bf16[64,384]{1,0:T(8,128)(2,1)S(1)}, bf16[64,384]{1,0:T(8,128)(2,1)S(1)}, u32[]{:S(2)}, u32[]{:S(2)}) collective-permute-start(bf16[64,384]{1,0:T(8,128)(2,1)S(1)} %get-tuple-element.25.own), channel_id=1, source_target_pairs={{0,16},{4,20},{8,24},{12,28},{16,0},{20,4},{24,8},{28,12},{1,17},{... | collective-permute-start | bytes 147464 | tf_op jit(solution)/shard_map/ppermute | solution.py:375
  23.2 4.2 %all-to-all-start = ((bf16[16,64,384]{2,1,0:T(8,128)(2,1)}), bf16[16,64,384]{2,1,0:T(8,128)(2,1)S(1)}, u32[]{:S(2)}, u32[]{:S(2)}) async-start(bf16[16,64,384]{2,1,0:T(8,128)(2,1)} %bitcast.2), calls=%async_computation | async-start | bytes 1572864 | tf_op jit(solution)/shard_map/all_to_all | solution.py:374
  27.4 0.0 copy-start.3
  27.5 0.0 copy-start.8
  27.5 1.4 %collective-permute-start.7 = (bf16[128,384]{1,0:T(8,128)(2,1)S(1)}, bf16[128,384]{1,0:T(8,128)(2,1)S(1)}, u32[]{:S(2)}, u32[]{:S(2)}) collective-permute-start(bf16[128,384]{1,0:T(8,128)(2,1)S(1)} %shard_map.113), channel_id=1, source_target_pairs={{0,8},{4,12},{8,0},{12,4},{16,24},{20,28},{24,16},{28,20},{1,9},{5... | collective-permute-start | bytes 294920 | tf_op jit(solution)/shard_map/ppermute | solution.py:376
  28.9 1.2 %collective-permute-start.6 = (bf16[128,384]{1,0:T(8,128)(2,1)S(1)}, bf16[128,384]{1,0:T(8,128)(2,1)S(1)}, u32[]{:S(2)}, u32[]{:S(2)}) collective-permute-start(bf16[128,384]{1,0:T(8,128)(2,1)S(1)} %shard_map.113), channel_id=1, source_target_pairs={{0,28},{4,0},{8,4},{12,8},{16,12},{20,16},{24,20},{28,24},{1,29},{... | collective-permute-start | bytes 294920 | tf_op jit(solution)/shard_map/ppermute | solution.py:376
  30.0 0.9 %collective-permute-start.5 = (bf16[128,384]{1,0:T(8,128)(2,1)S(1)}, bf16[128,384]{1,0:T(8,128)(2,1)S(1)}, u32[]{:S(2)}, u32[]{:S(2)}) collective-permute-start(bf16[128,384]{1,0:T(8,128)(2,1)S(1)} %shard_map.113), channel_id=1, source_target_pairs={{0,4},{4,8},{8,12},{12,16},{16,20},{20,24},{24,28},{28,0},{1,5},{5... | collective-permute-start | bytes 294920 | tf_op jit(solution)/shard_map/ppermute | solution.py:376
  30.9 2.4 %collective-permute-done.7 = bf16[128,384]{1,0:T(8,128)(2,1)S(1)} collective-permute-done((bf16[128,384]{1,0:T(8,128)(2,1)S(1)}, bf16[128,384]{1,0:T(8,128)(2,1)S(1)}, u32[]{:S(2)}, u32[]{:S(2)}) %collective-permute-start.7) | collective-permute-done | bytes 98336 | tf_op jit(solution)/shard_map/ppermute | solution.py:376
  33.3 2.5 %collective-permute-done.6 = bf16[128,384]{1,0:T(8,128)(2,1)S(1)} collective-permute-done((bf16[128,384]{1,0:T(8,128)(2,1)S(1)}, bf16[128,384]{1,0:T(8,128)(2,1)S(1)}, u32[]{:S(2)}, u32[]{:S(2)}) %collective-permute-start.6) | collective-permute-done | bytes 98336 | tf_op jit(solution)/shard_map/ppermute | solution.py:376
  35.8 0.1 collective-permute-start.8
  35.9 0.6 %shard_map.114 = (bf16[512,384]{1,0:T(8,128)(2,1)S(1)}, bf16[384,512]{1,0:T(8,128)(2,1)S(1)}) custom-call(bf16[512,384]{1,0:T(8,128)(2,1)S(1)} %pad_maximum_fusion.normed, bf16[384,1152]{1,0:T(8,128)(2,1)S(1)} %copy-done.1, f32[1152]{0:T(1024)S(1)} %copy-done.6), custom_call_target="tpu_custom_call" | custom-call | flops 1073741824 | bytes 1048576 | tf_op jit(solution)/shard_map/pallas_call | solution.py:253
  36.6 1.1 %collective-permute-done.8.other = bf16[512,384]{1,0:T(8,128)(2,1)S(1)} collective-permute-done((bf16[512,384]{1,0:T(8,128)(2,1)S(1)}, bf16[512,384]{1,0:T(8,128)(2,1)S(1)}, u32[]{:S(2)}, u32[]{:S(2)}) %collective-permute-start.8) | collective-permute-done | bytes 393248 | tf_op jit(solution)/shard_map/ppermute | solution.py:377
  37.7 3.4 %all-to-all-done = bf16[16,64,384]{2,1,0:T(8,128)(2,1)S(1)} async-done(((bf16[16,64,384]{2,1,0:T(8,128)(2,1)}), bf16[16,64,384]{2,1,0:T(8,128)(2,1)S(1)}, u32[]{:S(2)}, u32[]{:S(2)}) %all-to-all-start) | async-done | bytes 786464 | tf_op jit(solution)/shard_map/all_to_all | solution.py:374
  41.0 3.2 %shard_map.115 = bf16[16,200,128]{2,1,0:T(8,128)(2,1)S(1)} custom-call(bf16[1024,384]{1,0:T(8,128)(2,1)S(1)} %bitcast.7, bf16[512,384]{1,0:T(8,128)(2,1)S(1)} %get-tuple-element.26.line_keys, bf16[384,512]{1,0:T(8,128)(2,1)S(1)} %get-tuple-element.27.line_values, bf16[512,384]{1,0:T(8,128)(2,1)S(1)} %collective-permute-done.8.other, ...), custom_call_target="tpu_custom_call" | custom-call | tf_op jit(solution)/shard_map/pallas_call | solution.py:299
  44.2 18.1 %all_to_all.16.partials = bf16[16,200,128]{2,1,0:T(8,128)(2,1)S(1)} all-to-all(bf16[16,200,128]{2,1,0:T(8,128)(2,1)S(1)} %shard_map.115), channel_id=1, replica_groups=mesh['x'=4,'ylo'=2,'z'=8,'yhi'=2,'core'=2] {'x','yhi','ylo'}, dimensions={0} | all-to-all | bytes 1638400 | tf_op jit(solution)/shard_map/all_to_all | solution.py:385
  62.3 1.2 %shard_map.116 = bf16[64,384]{1,0:T(8,128)(2,1)} custom-call(bf16[16,200,128]{2,1,0:T(8,128)(2,1)S(1)} %all_to_all.16.partials, bf16[64,384]{1,0:T(8,128)(2,1)S(1)} %get-tuple-element.28.middle, bf16[384,384]{1,0:T(8,128)(2,1)S(1)} %copy-done.3, f32[384]{0:T(512)S(1)} %copy-done.8), custom_call_target="tpu_custom_call" | custom-call | tf_op jit(solution)/shard_map/pallas_call | solution.py:331
  (20 shorter events, 0.1 us)
Async XLA Ops:
  1.0 6.0 %collective-permute-start = (bf16[3,8,384]{2,1,0:T(8,128)(2,1)S(1)}, bf16[3,8,384]{2,1,0:T(8,128)(2,1)S(1)}, u32[]{:S(2)}, u32[]{:S(2)}) collective-permute-start(bf16[3,8,384]{2,1,0:T(8,128)(2,1)S(1)} %get-tuple-element.17), channel_id=1, source_target_pairs={{0,224},{32,64},{64,32},{96,128},{128,96},{160,192},{192,160},{224... | collective-permute-start | bytes 55304 | tf_op jit(solution)/shard_map/ppermute | solution.py:33
  4.9 3.8 %collective-permute-start.1 = (bf16[3,8,384]{2,1,0:T(8,128)(2,1)S(1)}, bf16[3,8,384]{2,1,0:T(8,128)(2,1)S(1)}, u32[]{:S(2)}, u32[]{:S(2)}) collective-permute-start(bf16[3,8,384]{2,1,0:T(8,128)(2,1)S(1)} %get-tuple-element.18), channel_id=1, source_target_pairs={{0,32},{32,0},{64,96},{96,64},{128,160},{160,128},{192,224},{224,1... | collective-permute-start | bytes 55304 | tf_op jit(solution)/shard_map/ppermute | solution.py:34
  8.6 3.3 %copy-start = (bf16[27,384,384]{2,1,0:T(8,128)(2,1)S(1)}, bf16[27,384,384]{2,1,0:T(8,128)(2,1)}, u32[]{:S(2)}) copy-start(bf16[27,384,384]{2,1,0:T(8,128)(2,1)} %param.15) | copy-start | bytes 23887876
  8.6 3.3 %copy-start.2 = (bf16[2,8,8,384]{3,2,1,0:T(8,128)(2,1)S(1)}, bf16[2,8,8,384]{3,2,1,0:T(8,128)(2,1)}, u32[]{:S(2)}) copy-start(bf16[2,8,8,384]{3,2,1,0:T(8,128)(2,1)} %cache.1) | copy-start | bytes 294916
  8.6 3.3 %copy-start.4 = (bf16[8,8,384]{2,1,0:T(8,128)(2,1)S(1)}, bf16[8,8,384]{2,1,0:T(8,128)(2,1)}, u32[]{:S(2)}) copy-start(bf16[8,8,384]{2,1,0:T(8,128)(2,1)} %hidden.1) | copy-start | bytes 147460
  8.6 3.3 %copy-start.7 = (f32[384]{0:T(512)S(1)}, f32[384]{0:T(512)}, u32[]{:S(2)}) copy-start(f32[384]{0:T(512)} %norm_gain.3) | copy-start | bytes 4612
  8.7 5.9 %copy-start.1 = (bf16[384,1152]{1,0:T(8,128)(2,1)S(1)}, bf16[384,1152]{1,0:T(8,128)(2,1)}, u32[]{:S(2)}) copy-start(bf16[384,1152]{1,0:T(8,128)(2,1)} %w_qkv.5) | copy-start | bytes 2654212
  8.7 5.9 %copy-start.5 = (bf16[8,8,384]{2,1,0:T(8,128)(2,1)S(1)}, bf16[8,8,384]{2,1,0:T(8,128)(2,1)}, u32[]{:S(2)}) copy-start(bf16[8,8,384]{2,1,0:T(8,128)(2,1)} %param.12) | copy-start | bytes 147460
  8.7 5.9 %copy-start.6 = (f32[1152]{0:T(1024)S(1)}, f32[1152]{0:T(1024)}, u32[]{:S(2)}) copy-start(f32[1152]{0:T(1024)} %b_qkv.5) | copy-start | bytes 13828
  8.7 5.9 %copy-start.9 = (f32[384]{0:T(512)S(1)}, f32[384]{0:T(512)}, u32[]{:S(2)}) copy-start(f32[384]{0:T(512)} %conv_bias.1) | copy-start | bytes 4612
  8.7 5.9 %copy-start.10 = (f32[384]{0:T(512)S(1)}, f32[384]{0:T(512)}, u32[]{:S(2)}) copy-start(f32[384]{0:T(512)} %attn_gain.1) | copy-start | bytes 4612
  8.8 5.9 %collective-permute-start.2 = (bf16[3,10,384]{2,1,0:T(8,128)(2,1)S(1)}, bf16[3,10,384]{2,1,0:T(8,128)(2,1)S(1)}, u32[]{:S(2)}, u32[]{:S(2)}) collective-permute-start(bf16[3,10,384]{2,1,0:T(8,128)(2,1)S(1)} %get-tuple-element.22), channel_id=1, source_target_pairs={{0,31},{1,2},{2,1},{3,4},{4,3},{5,6},{6,5},{7,8},{8,7},{9,10},{10,... | collective-permute-start | bytes 69128 | tf_op jit(solution)/shard_map/ppermute | solution.py:33
  9.6 5.0 %collective-permute-start.3 = (bf16[3,10,384]{2,1,0:T(8,128)(2,1)S(1)}, bf16[3,10,384]{2,1,0:T(8,128)(2,1)S(1)}, u32[]{:S(2)}, u32[]{:S(2)}) collective-permute-start(bf16[3,10,384]{2,1,0:T(8,128)(2,1)S(1)} %get-tuple-element.23), channel_id=1, source_target_pairs={{0,1},{1,0},{2,3},{3,2},{4,5},{5,4},{6,7},{7,6},{8,9},{9,8},{10,11... | collective-permute-start | bytes 69128 | tf_op jit(solution)/shard_map/ppermute | solution.py:34
  16.9 10.5 %collective-permute-start.4 = (bf16[64,384]{1,0:T(8,128)(2,1)S(1)}, bf16[64,384]{1,0:T(8,128)(2,1)S(1)}, u32[]{:S(2)}, u32[]{:S(2)}) collective-permute-start(bf16[64,384]{1,0:T(8,128)(2,1)S(1)} %get-tuple-element.25.own), channel_id=1, source_target_pairs={{0,16},{4,20},{8,24},{12,28},{16,0},{20,4},{24,8},{28,12},{1,17},{... | collective-permute-start | bytes 147464 | tf_op jit(solution)/shard_map/ppermute | solution.py:375
  23.2 17.8 %all-to-all-start = ((bf16[16,64,384]{2,1,0:T(8,128)(2,1)}), bf16[16,64,384]{2,1,0:T(8,128)(2,1)S(1)}, u32[]{:S(2)}, u32[]{:S(2)}) async-start(bf16[16,64,384]{2,1,0:T(8,128)(2,1)} %bitcast.2), calls=%async_computation | async-start | bytes 1572864 | tf_op jit(solution)/shard_map/all_to_all | solution.py:374
  27.4 34.9 %copy-start.3 = (bf16[384,384]{1,0:T(8,128)(2,1)S(1)}, bf16[384,384]{1,0:T(8,128)(2,1)}, u32[]{:S(2)}) copy-start(bf16[384,384]{1,0:T(8,128)(2,1)} %w_proj.1) | copy-start | bytes 884740
  27.5 34.9 %copy-start.8 = (f32[384]{0:T(512)S(1)}, f32[384]{0:T(512)}, u32[]{:S(2)}) copy-start(f32[384]{0:T(512)} %b_proj.1) | copy-start | bytes 4612
  27.5 5.8 %collective-permute-start.7 = (bf16[128,384]{1,0:T(8,128)(2,1)S(1)}, bf16[128,384]{1,0:T(8,128)(2,1)S(1)}, u32[]{:S(2)}, u32[]{:S(2)}) collective-permute-start(bf16[128,384]{1,0:T(8,128)(2,1)S(1)} %shard_map.113), channel_id=1, source_target_pairs={{0,8},{4,12},{8,0},{12,4},{16,24},{20,28},{24,16},{28,20},{1,9},{5... | collective-permute-start | bytes 294920 | tf_op jit(solution)/shard_map/ppermute | solution.py:376
  28.9 6.9 %collective-permute-start.6 = (bf16[128,384]{1,0:T(8,128)(2,1)S(1)}, bf16[128,384]{1,0:T(8,128)(2,1)S(1)}, u32[]{:S(2)}, u32[]{:S(2)}) collective-permute-start(bf16[128,384]{1,0:T(8,128)(2,1)S(1)} %shard_map.113), channel_id=1, source_target_pairs={{0,28},{4,0},{8,4},{12,8},{16,12},{20,16},{24,20},{28,24},{1,29},{... | collective-permute-start | bytes 294920 | tf_op jit(solution)/shard_map/ppermute | solution.py:376
  30.0 5.8 %collective-permute-start.5 = (bf16[128,384]{1,0:T(8,128)(2,1)S(1)}, bf16[128,384]{1,0:T(8,128)(2,1)S(1)}, u32[]{:S(2)}, u32[]{:S(2)}) collective-permute-start(bf16[128,384]{1,0:T(8,128)(2,1)S(1)} %shard_map.113), channel_id=1, source_target_pairs={{0,4},{4,8},{8,12},{12,16},{16,20},{20,24},{24,28},{28,0},{1,5},{5... | collective-permute-start | bytes 294920 | tf_op jit(solution)/shard_map/ppermute | solution.py:376
  35.8 1.8 %collective-permute-start.8 = (bf16[512,384]{1,0:T(8,128)(2,1)S(1)}, bf16[512,384]{1,0:T(8,128)(2,1)S(1)}, u32[]{:S(2)}, u32[]{:S(2)}) collective-permute-start(bf16[512,384]{1,0:T(8,128)(2,1)S(1)} %pad_maximum_fusion.normed), channel_id=1, source_target_pairs={{0,1},{1,0},{2,3},{3,2},{4,5},{5,4},{6,7},{7,6},{8,9},{9,8},{10,11... | collective-permute-start | bytes 1179656 | tf_op jit(solution)/shard_map/ppermute | solution.py:377

commit v6 on v5

--- a/solution.py
+++ b/solution.py
@@ -65,8 +65,11 @@
 
 def edge_kernel(cache_h, hidden_h, outer, inner, sides, cache, hidden, wide, sems):
     odd = lax.axis_index("ylo")
-    arrive(fetch(((cache_h, cache), (hidden_h, hidden)), sems))
+    arriving = fetch(
+        ((cache_h.at[0], cache.at[0]), (cache_h.at[1], cache.at[1]), (hidden_h, hidden)), sems
+    )
     for frame in range(3):
+        arriving[frame].wait()
         own = (cache[frame] if frame < 2 else hidden[...]).astype(F32)
         wide[...] = own
         outer[frame] = jnp.where(odd == 1, own[TILE - 1], own[0]).astype(BF16)
@@ -85,7 +88,7 @@
             pltpu.VMEM((2, TILE, TILE, C), BF16),
             pltpu.VMEM((TILE, TILE, C), BF16),
             pltpu.VMEM((TILE, TILE, C), F32),
-            pltpu.SemaphoreType.DMA((2,)),
+            pltpu.SemaphoreType.DMA((3,)),
         ],
         compiler_params=pltpu.CompilerParams(vmem_limit_bytes=55120 << 10),
     )(cache, hidden)

time: 63.7 us -> 63.7 us (level)
  no operation moved by 1% of the time
where the time goes in v6:
time: 63.7 us; the launch traced here: 63.4 us
  starting transfers between devices  21 us (33%)
  blocking collectives  18.1 us (28%)
  waiting for transfers between devices  15.3 us (24%)
  Pallas kernels  8.76 us (14%)
    all_to_all x1, blocking collectives, shards(): partials = lax.all_to_all(partial, PLANE, 0, 0, tiled=True)  18.1 us
    ppermute x1, starting transfers between devices, shards(): far = pair_stage(normed, lax.ppermute(normed, 'z', flips(4)))  6.29 us
    ppermute x3, waiting for transfers between devices, shards(): lax.ppermute(far, 'z', links)  4.9 us
    ppermute x2, starting transfers between devices, swapped(): far = lax.ppermute(edges[1], axes, outer)  4.74 us
    ppermute x2, waiting for transfers between devices, swapped(): far = lax.ppermute(edges[1], axes, outer)  4.27 us
    all_to_all x1, starting transfers between devices, shards(): all_queries = lax.all_to_all(queries, PLANE, 0, 0, tiled=True)  4.2 us
    ppermute x3, starting transfers between devices, shards(): lax.ppermute(far, 'z', links)  3.43 us
    all_to_all x1, waiting for transfers between devices, shards(): all_queries = lax.all_to_all(queries, PLANE, 0, 0, tiled=True)  3.39 us
  transfers between devices with their start and end apart: 10, of which 7 were waited for; matrix products, arithmetic and copies ran while one was open for 0% of the time, Pallas kernels for 2%

profile of v6, /device:TPU:32, one launch (start us, length us, event | category | flops | bytes accessed | tf_op | source)
XLA Modules:
  0.0 63.4 jit_solution(16267637173504430930)
XLA Ops:
  0.0 0.9 %shard_map.109 = (bf16[3,8,384]{2,1,0:T(8,128)(2,1)S(1)}, bf16[3,8,384]{2,1,0:T(8,128)(2,1)S(1)}, bf16[2,3,8,384]{3,2,1,0:T(8,128)(2,1)S(1)}) custom-call(bf16[2,8,8,384]{3,2,1,0:T(8,128)(2,1)} %cache.1, bf16[8,8,384]{2,1,0:T(8,128)(2,1)} %hidden.1), custom_call_target="tpu_custom_call" | custom-call | tf_op jit(solution)/shard_map/pallas_call | solution.py:83
  0.9 3.9 %collective-permute-start = (bf16[3,8,384]{2,1,0:T(8,128)(2,1)S(1)}, bf16[3,8,384]{2,1,0:T(8,128)(2,1)S(1)}, u32[]{:S(2)}, u32[]{:S(2)}) collective-permute-start(bf16[3,8,384]{2,1,0:T(8,128)(2,1)S(1)} %get-tuple-element.17), channel_id=1, source_target_pairs={{0,224},{32,64},{64,32},{96,128},{128,96},{160,192},{192,160},{224... | collective-permute-start | bytes 55304 | tf_op jit(solution)/shard_map/ppermute | solution.py:33
  4.8 0.0 collective-permute-start.1
  4.8 2.1 %collective-permute-done.row_outer = bf16[3,8,384]{2,1,0:T(8,128)(2,1)S(1)} collective-permute-done((bf16[3,8,384]{2,1,0:T(8,128)(2,1)S(1)}, bf16[3,8,384]{2,1,0:T(8,128)(2,1)S(1)}, u32[]{:S(2)}, u32[]{:S(2)}) %collective-permute-start) | collective-permute-done | bytes 18464 | tf_op jit(solution)/shard_map/ppermute | solution.py:33
  6.9 1.7 %collective-permute-done.1.row_inner = bf16[3,8,384]{2,1,0:T(8,128)(2,1)S(1)} collective-permute-done((bf16[3,8,384]{2,1,0:T(8,128)(2,1)S(1)}, bf16[3,8,384]{2,1,0:T(8,128)(2,1)S(1)}, u32[]{:S(2)}, u32[]{:S(2)}) %collective-permute-start.1) | collective-permute-done | bytes 18464 | tf_op jit(solution)/shard_map/ppermute | solution.py:34
  8.6 0.0 copy-start.1
  8.6 0.0 copy-start.5
  8.6 0.0 copy-start.6
  8.7 0.0 copy-start.9
  8.7 0.0 copy-start.10
  8.7 0.9 %collective-permute-start.2 = (bf16[3,10,384]{2,1,0:T(8,128)(2,1)S(1)}, bf16[3,10,384]{2,1,0:T(8,128)(2,1)S(1)}, u32[]{:S(2)}, u32[]{:S(2)}) collective-permute-start(bf16[3,10,384]{2,1,0:T(8,128)(2,1)S(1)} %get-tuple-element.22), channel_id=1, source_target_pairs={{0,31},{1,2},{2,1},{3,4},{4,3},{5,6},{6,5},{7,8},{8,7},{9,10},{10,... | collective-permute-start | bytes 69128 | tf_op jit(solution)/shard_map/ppermute | solution.py:33
  9.6 2.2 %collective-permute-start.3 = (bf16[3,10,384]{2,1,0:T(8,128)(2,1)S(1)}, bf16[3,10,384]{2,1,0:T(8,128)(2,1)S(1)}, u32[]{:S(2)}, u32[]{:S(2)}) collective-permute-start(bf16[3,10,384]{2,1,0:T(8,128)(2,1)S(1)} %get-tuple-element.23), channel_id=1, source_target_pairs={{0,1},{1,0},{2,3},{3,2},{4,5},{5,4},{6,7},{7,6},{8,9},{9,8},{10,11... | collective-permute-start | bytes 69128 | tf_op jit(solution)/shard_map/ppermute | solution.py:34
  11.8 0.0 copy-done
  11.8 0.5 shard_map.110
  12.4 2.2 %collective-permute-done.2.col_outer = bf16[3,10,384]{2,1,0:T(8,128)(2,1)S(1)} collective-permute-done((bf16[3,10,384]{2,1,0:T(8,128)(2,1)S(1)}, bf16[3,10,384]{2,1,0:T(8,128)(2,1)S(1)}, u32[]{:S(2)}, u32[]{:S(2)}) %collective-permute-start.2) | collective-permute-done | bytes 23072 | tf_op jit(solution)/shard_map/ppermute | solution.py:33
  14.6 2.2 %shard_map.112 = (bf16[64,384]{1,0:T(8,128)(2,1)S(1)}, bf16[64,384]{1,0:T(8,128)(2,1)S(1)}, bf16[1024,384]{1,0:T(8,128)(2,1)}) custom-call(f32[64,384]{1,0:T(8,128)S(1)} %get-tuple-element.19.centre, f32[3,10,8,384]{3,2,1,0:T(8,128)S(1)} %get-tuple-element.20.tall, bf16[3,10,384]{2,1,0:T(8,128)(2,1)S(1)} %collective-permute-done.2.col_outer, ...), custom_call_target="tpu_custom_call" | custom-call | tf_op jit(solution)/shard_map/pallas_call | solution.py:214
  16.8 6.3 %collective-permute-start.4 = (bf16[64,384]{1,0:T(8,128)(2,1)S(1)}, bf16[64,384]{1,0:T(8,128)(2,1)S(1)}, u32[]{:S(2)}, u32[]{:S(2)}) collective-permute-start(bf16[64,384]{1,0:T(8,128)(2,1)S(1)} %get-tuple-element.25.own), channel_id=1, source_target_pairs={{0,16},{4,20},{8,24},{12,28},{16,0},{20,4},{24,8},{28,12},{1,17},{... | collective-permute-start | bytes 147464 | tf_op jit(solution)/shard_map/ppermute | solution.py:378
  23.1 4.2 %all-to-all-start = ((bf16[16,64,384]{2,1,0:T(8,128)(2,1)}), bf16[16,64,384]{2,1,0:T(8,128)(2,1)S(1)}, u32[]{:S(2)}, u32[]{:S(2)}) async-start(bf16[16,64,384]{2,1,0:T(8,128)(2,1)} %bitcast.2), calls=%async_computation | async-start | bytes 1572864 | tf_op jit(solution)/shard_map/all_to_all | solution.py:377
  27.4 0.0 copy-start.3
  27.4 0.0 copy-start.8
  27.4 1.4 %collective-permute-start.7 = (bf16[128,384]{1,0:T(8,128)(2,1)S(1)}, bf16[128,384]{1,0:T(8,128)(2,1)S(1)}, u32[]{:S(2)}, u32[]{:S(2)}) collective-permute-start(bf16[128,384]{1,0:T(8,128)(2,1)S(1)} %shard_map.113), channel_id=1, source_target_pairs={{0,8},{4,12},{8,0},{12,4},{16,24},{20,28},{24,16},{28,20},{1,9},{5... | collective-permute-start | bytes 294920 | tf_op jit(solution)/shard_map/ppermute | solution.py:379
  28.8 1.2 %collective-permute-start.6 = (bf16[128,384]{1,0:T(8,128)(2,1)S(1)}, bf16[128,384]{1,0:T(8,128)(2,1)S(1)}, u32[]{:S(2)}, u32[]{:S(2)}) collective-permute-start(bf16[128,384]{1,0:T(8,128)(2,1)S(1)} %shard_map.113), channel_id=1, source_target_pairs={{0,28},{4,0},{8,4},{12,8},{16,12},{20,16},{24,20},{28,24},{1,29},{... | collective-permute-start | bytes 294920 | tf_op jit(solution)/shard_map/ppermute | solution.py:379
  30.0 0.9 %collective-permute-start.5 = (bf16[128,384]{1,0:T(8,128)(2,1)S(1)}, bf16[128,384]{1,0:T(8,128)(2,1)S(1)}, u32[]{:S(2)}, u32[]{:S(2)}) collective-permute-start(bf16[128,384]{1,0:T(8,128)(2,1)S(1)} %shard_map.113), channel_id=1, source_target_pairs={{0,4},{4,8},{8,12},{12,16},{16,20},{20,24},{24,28},{28,0},{1,5},{5... | collective-permute-start | bytes 294920 | tf_op jit(solution)/shard_map/ppermute | solution.py:379
  30.8 2.4 %collective-permute-done.7 = bf16[128,384]{1,0:T(8,128)(2,1)S(1)} collective-permute-done((bf16[128,384]{1,0:T(8,128)(2,1)S(1)}, bf16[128,384]{1,0:T(8,128)(2,1)S(1)}, u32[]{:S(2)}, u32[]{:S(2)}) %collective-permute-start.7) | collective-permute-done | bytes 98336 | tf_op jit(solution)/shard_map/ppermute | solution.py:379
  33.2 2.5 %collective-permute-done.6 = bf16[128,384]{1,0:T(8,128)(2,1)S(1)} collective-permute-done((bf16[128,384]{1,0:T(8,128)(2,1)S(1)}, bf16[128,384]{1,0:T(8,128)(2,1)S(1)}, u32[]{:S(2)}, u32[]{:S(2)}) %collective-permute-start.6) | collective-permute-done | bytes 98336 | tf_op jit(solution)/shard_map/ppermute | solution.py:379
  35.8 0.1 collective-permute-start.8
  35.9 0.6 %shard_map.114 = (bf16[512,384]{1,0:T(8,128)(2,1)S(1)}, bf16[384,512]{1,0:T(8,128)(2,1)S(1)}) custom-call(bf16[512,384]{1,0:T(8,128)(2,1)S(1)} %pad_maximum_fusion.normed, bf16[384,1152]{1,0:T(8,128)(2,1)S(1)} %copy-done.1, f32[1152]{0:T(1024)S(1)} %copy-done.6), custom_call_target="tpu_custom_call" | custom-call | flops 1073741824 | bytes 1048576 | tf_op jit(solution)/shard_map/pallas_call | solution.py:256
  36.5 1.1 %collective-permute-done.8.other = bf16[512,384]{1,0:T(8,128)(2,1)S(1)} collective-permute-done((bf16[512,384]{1,0:T(8,128)(2,1)S(1)}, bf16[512,384]{1,0:T(8,128)(2,1)S(1)}, u32[]{:S(2)}, u32[]{:S(2)}) %collective-permute-start.8) | collective-permute-done | bytes 393248 | tf_op jit(solution)/shard_map/ppermute | solution.py:380
  37.6 3.4 %all-to-all-done = bf16[16,64,384]{2,1,0:T(8,128)(2,1)S(1)} async-done(((bf16[16,64,384]{2,1,0:T(8,128)(2,1)}), bf16[16,64,384]{2,1,0:T(8,128)(2,1)S(1)}, u32[]{:S(2)}, u32[]{:S(2)}) %all-to-all-start) | async-done | bytes 786464 | tf_op jit(solution)/shard_map/all_to_all | solution.py:377
  41.0 3.2 %shard_map.115 = bf16[16,200,128]{2,1,0:T(8,128)(2,1)S(1)} custom-call(bf16[1024,384]{1,0:T(8,128)(2,1)S(1)} %bitcast.7, bf16[512,384]{1,0:T(8,128)(2,1)S(1)} %get-tuple-element.26.line_keys, bf16[384,512]{1,0:T(8,128)(2,1)S(1)} %get-tuple-element.27.line_values, bf16[512,384]{1,0:T(8,128)(2,1)S(1)} %collective-permute-done.8.other, ...), custom_call_target="tpu_custom_call" | custom-call | tf_op jit(solution)/shard_map/pallas_call | solution.py:302
  44.1 18.1 %all_to_all.16.partials = bf16[16,200,128]{2,1,0:T(8,128)(2,1)S(1)} all-to-all(bf16[16,200,128]{2,1,0:T(8,128)(2,1)S(1)} %shard_map.115), channel_id=1, replica_groups=mesh['x'=4,'ylo'=2,'z'=8,'yhi'=2,'core'=2] {'x','yhi','ylo'}, dimensions={0} | all-to-all | bytes 1638400 | tf_op jit(solution)/shard_map/all_to_all | solution.py:388
  62.2 1.2 %shard_map.116 = bf16[64,384]{1,0:T(8,128)(2,1)} custom-call(bf16[16,200,128]{2,1,0:T(8,128)(2,1)S(1)} %all_to_all.16.partials, bf16[64,384]{1,0:T(8,128)(2,1)S(1)} %get-tuple-element.28.middle, bf16[384,384]{1,0:T(8,128)(2,1)S(1)} %copy-done.3, f32[384]{0:T(512)S(1)} %copy-done.8), custom_call_target="tpu_custom_call" | custom-call | tf_op jit(solution)/shard_map/pallas_call | solution.py:334
  (20 shorter events, 0.1 us)
Async XLA Ops:
  0.9 6.0 %collective-permute-start = (bf16[3,8,384]{2,1,0:T(8,128)(2,1)S(1)}, bf16[3,8,384]{2,1,0:T(8,128)(2,1)S(1)}, u32[]{:S(2)}, u32[]{:S(2)}) collective-permute-start(bf16[3,8,384]{2,1,0:T(8,128)(2,1)S(1)} %get-tuple-element.17), channel_id=1, source_target_pairs={{0,224},{32,64},{64,32},{96,128},{128,96},{160,192},{192,160},{224... | collective-permute-start | bytes 55304 | tf_op jit(solution)/shard_map/ppermute | solution.py:33
  4.8 3.8 %collective-permute-start.1 = (bf16[3,8,384]{2,1,0:T(8,128)(2,1)S(1)}, bf16[3,8,384]{2,1,0:T(8,128)(2,1)S(1)}, u32[]{:S(2)}, u32[]{:S(2)}) collective-permute-start(bf16[3,8,384]{2,1,0:T(8,128)(2,1)S(1)} %get-tuple-element.18), channel_id=1, source_target_pairs={{0,32},{32,0},{64,96},{96,64},{128,160},{160,128},{192,224},{224,1... | collective-permute-start | bytes 55304 | tf_op jit(solution)/shard_map/ppermute | solution.py:34
  8.6 3.3 %copy-start = (bf16[27,384,384]{2,1,0:T(8,128)(2,1)S(1)}, bf16[27,384,384]{2,1,0:T(8,128)(2,1)}, u32[]{:S(2)}) copy-start(bf16[27,384,384]{2,1,0:T(8,128)(2,1)} %param.15) | copy-start | bytes 23887876
  8.6 3.3 %copy-start.2 = (bf16[2,8,8,384]{3,2,1,0:T(8,128)(2,1)S(1)}, bf16[2,8,8,384]{3,2,1,0:T(8,128)(2,1)}, u32[]{:S(2)}) copy-start(bf16[2,8,8,384]{3,2,1,0:T(8,128)(2,1)} %cache.1) | copy-start | bytes 294916
  8.6 3.3 %copy-start.4 = (bf16[8,8,384]{2,1,0:T(8,128)(2,1)S(1)}, bf16[8,8,384]{2,1,0:T(8,128)(2,1)}, u32[]{:S(2)}) copy-start(bf16[8,8,384]{2,1,0:T(8,128)(2,1)} %hidden.1) | copy-start | bytes 147460
  8.6 3.3 %copy-start.7 = (f32[384]{0:T(512)S(1)}, f32[384]{0:T(512)}, u32[]{:S(2)}) copy-start(f32[384]{0:T(512)} %norm_gain.3) | copy-start | bytes 4612
  8.6 5.9 %copy-start.1 = (bf16[384,1152]{1,0:T(8,128)(2,1)S(1)}, bf16[384,1152]{1,0:T(8,128)(2,1)}, u32[]{:S(2)}) copy-start(bf16[384,1152]{1,0:T(8,128)(2,1)} %w_qkv.5) | copy-start | bytes 2654212
  8.6 5.9 %copy-start.5 = (bf16[8,8,384]{2,1,0:T(8,128)(2,1)S(1)}, bf16[8,8,384]{2,1,0:T(8,128)(2,1)}, u32[]{:S(2)}) copy-start(bf16[8,8,384]{2,1,0:T(8,128)(2,1)} %param.12) | copy-start | bytes 147460
  8.6 5.9 %copy-start.6 = (f32[1152]{0:T(1024)S(1)}, f32[1152]{0:T(1024)}, u32[]{:S(2)}) copy-start(f32[1152]{0:T(1024)} %b_qkv.5) | copy-start | bytes 13828
  8.7 5.9 %copy-start.9 = (f32[384]{0:T(512)S(1)}, f32[384]{0:T(512)}, u32[]{:S(2)}) copy-start(f32[384]{0:T(512)} %conv_bias.1) | copy-start | bytes 4612
  8.7 5.9 %copy-start.10 = (f32[384]{0:T(512)S(1)}, f32[384]{0:T(512)}, u32[]{:S(2)}) copy-start(f32[384]{0:T(512)} %attn_gain.1) | copy-start | bytes 4612
  8.7 5.9 %collective-permute-start.2 = (bf16[3,10,384]{2,1,0:T(8,128)(2,1)S(1)}, bf16[3,10,384]{2,1,0:T(8,128)(2,1)S(1)}, u32[]{:S(2)}, u32[]{:S(2)}) collective-permute-start(bf16[3,10,384]{2,1,0:T(8,128)(2,1)S(1)} %get-tuple-element.22), channel_id=1, source_target_pairs={{0,31},{1,2},{2,1},{3,4},{4,3},{5,6},{6,5},{7,8},{8,7},{9,10},{10,... | collective-permute-start | bytes 69128 | tf_op jit(solution)/shard_map/ppermute | solution.py:33
  9.6 5.0 %collective-permute-start.3 = (bf16[3,10,384]{2,1,0:T(8,128)(2,1)S(1)}, bf16[3,10,384]{2,1,0:T(8,128)(2,1)S(1)}, u32[]{:S(2)}, u32[]{:S(2)}) collective-permute-start(bf16[3,10,384]{2,1,0:T(8,128)(2,1)S(1)} %get-tuple-element.23), channel_id=1, source_target_pairs={{0,1},{1,0},{2,3},{3,2},{4,5},{5,4},{6,7},{7,6},{8,9},{9,8},{10,11... | collective-permute-start | bytes 69128 | tf_op jit(solution)/shard_map/ppermute | solution.py:34
  16.8 10.5 %collective-permute-start.4 = (bf16[64,384]{1,0:T(8,128)(2,1)S(1)}, bf16[64,384]{1,0:T(8,128)(2,1)S(1)}, u32[]{:S(2)}, u32[]{:S(2)}) collective-permute-start(bf16[64,384]{1,0:T(8,128)(2,1)S(1)} %get-tuple-element.25.own), channel_id=1, source_target_pairs={{0,16},{4,20},{8,24},{12,28},{16,0},{20,4},{24,8},{28,12},{1,17},{... | collective-permute-start | bytes 147464 | tf_op jit(solution)/shard_map/ppermute | solution.py:378
  23.1 17.8 %all-to-all-start = ((bf16[16,64,384]{2,1,0:T(8,128)(2,1)}), bf16[16,64,384]{2,1,0:T(8,128)(2,1)S(1)}, u32[]{:S(2)}, u32[]{:S(2)}) async-start(bf16[16,64,384]{2,1,0:T(8,128)(2,1)} %bitcast.2), calls=%async_computation | async-start | bytes 1572864 | tf_op jit(solution)/shard_map/all_to_all | solution.py:377
  27.4 34.9 %copy-start.3 = (bf16[384,384]{1,0:T(8,128)(2,1)S(1)}, bf16[384,384]{1,0:T(8,128)(2,1)}, u32[]{:S(2)}) copy-start(bf16[384,384]{1,0:T(8,128)(2,1)} %w_proj.1) | copy-start | bytes 884740
  27.4 34.9 %copy-start.8 = (f32[384]{0:T(512)S(1)}, f32[384]{0:T(512)}, u32[]{:S(2)}) copy-start(f32[384]{0:T(512)} %b_proj.1) | copy-start | bytes 4612
  27.4 5.8 %collective-permute-start.7 = (bf16[128,384]{1,0:T(8,128)(2,1)S(1)}, bf16[128,384]{1,0:T(8,128)(2,1)S(1)}, u32[]{:S(2)}, u32[]{:S(2)}) collective-permute-start(bf16[128,384]{1,0:T(8,128)(2,1)S(1)} %shard_map.113), channel_id=1, source_target_pairs={{0,8},{4,12},{8,0},{12,4},{16,24},{20,28},{24,16},{28,20},{1,9},{5... | collective-permute-start | bytes 294920 | tf_op jit(solution)/shard_map/ppermute | solution.py:379
  28.8 6.9 %collective-permute-start.6 = (bf16[128,384]{1,0:T(8,128)(2,1)S(1)}, bf16[128,384]{1,0:T(8,128)(2,1)S(1)}, u32[]{:S(2)}, u32[]{:S(2)}) collective-permute-start(bf16[128,384]{1,0:T(8,128)(2,1)S(1)} %shard_map.113), channel_id=1, source_target_pairs={{0,28},{4,0},{8,4},{12,8},{16,12},{20,16},{24,20},{28,24},{1,29},{... | collective-permute-start | bytes 294920 | tf_op jit(solution)/shard_map/ppermute | solution.py:379
  30.0 5.8 %collective-permute-start.5 = (bf16[128,384]{1,0:T(8,128)(2,1)S(1)}, bf16[128,384]{1,0:T(8,128)(2,1)S(1)}, u32[]{:S(2)}, u32[]{:S(2)}) collective-permute-start(bf16[128,384]{1,0:T(8,128)(2,1)S(1)} %shard_map.113), channel_id=1, source_target_pairs={{0,4},{4,8},{8,12},{12,16},{16,20},{20,24},{24,28},{28,0},{1,5},{5... | collective-permute-start | bytes 294920 | tf_op jit(solution)/shard_map/ppermute | solution.py:379
  35.8 1.8 %collective-permute-start.8 = (bf16[512,384]{1,0:T(8,128)(2,1)S(1)}, bf16[512,384]{1,0:T(8,128)(2,1)S(1)}, u32[]{:S(2)}, u32[]{:S(2)}) collective-permute-start(bf16[512,384]{1,0:T(8,128)(2,1)S(1)} %pad_maximum_fusion.normed), channel_id=1, source_target_pairs={{0,1},{1,0},{2,3},{3,2},{4,5},{5,4},{6,7},{7,6},{8,9},{9,8},{10,11... | collective-permute-start | bytes 1179656 | tf_op jit(solution)/shard_map/ppermute | solution.py:380
